TPU v7x, 1024 devices: a whole 4x4x32 slice. The times are simulated.
1024 devices in a mesh: gx: 64 (over y_hi, z), gy: 16 (over x, y_lo, core).
Axes of the slice: x: 4, y: 4 (y_hi: 2, y_lo: 2; y = y_hi * 2 + y_lo), z: 32, core: 2. Of those that a mesh axis runs over, the one named last changes fastest.
Arguments:
- state: bfloat16 [128, 16, 128, 256], P('gx', 'gy'), may hold values from -6 to 6
- species: int32 [128, 16, 128], P('gx', 'gy'), may hold values from 0 to 3
- species_bias: float32 [4, 256], replicated, may hold values from -4 to 4
- edge_index: int32 [128, 16, 2, 512], P('gx', 'gy'), may hold values from 0 to 1151, as said below
- edge_count: int32 [128, 16], P('gx', 'gy'), may hold values from 128 to 512, as said below
- edge_dist: float32 [128, 16, 512], P('gx', 'gy'), may hold values from 0.2 to 0.9
- trip_index: int32 [128, 16, 2, 1024], P('gx', 'gy'), may hold values from 0 to 511, as said below
- trip_count: int32 [128, 16], P('gx', 'gy'), may hold values from 256 to 1024, as said below
- trip_cos: float32 [128, 16, 1024], P('gx', 'gy'), may hold values from -1 to 1
- radial_weight: float32 [256], replicated, may hold values from -4 to 4
- norm_gain: float32 [256], replicated, may hold values from 0.1 to 1.9
- w_centre: bfloat16 [256, 256], replicated, may hold values from -0.375 to 0.375
- w_neigh: bfloat16 [256, 256], replicated, may hold values from -0.375 to 0.375
- w_mix: bfloat16 [256, 256], replicated, may hold values from -0.375 to 0.375
- w_out: bfloat16 [256, 256], replicated, may hold values from -0.375 to 0.375
Outputs:
- updated: bfloat16 [128, 16, 128, 256], P('gx', 'gy')
Inputs may be any that keep to these rules, and one draw needn't show every extreme that they name: `edge_index`: row 0 holds centre slots below 128; row 1 holds neighbour codes cell * 128 + slot with cell from 0 to 8 and slot below 128; slots at or past the tile's edge_count are padding of arbitrary such values. `edge_count`: some tile has all 512 slots live. `trip_index`: in live slots both rows name live edges of the same tile and differ; padding slots follow the same rule. `trip_count`: some tile has all 1024 slots live.
All inputs are finite; a program needn't handle non-finite values.
Results may differ from a plain program's by a relative error of at most 0.019.
Values may be sent and summed in bfloat16 or wider, within the bound.
No kernel may reach another device: no remote copies, remote signals or barrier semaphores. Data moves between devices by JAX's collectives and lax.ppermute only.
A program may use at most 32 MiB of HBM per device.

v0:
```python
import jax
import jax.numpy as jnp
from jax import lax
from jax.sharding import PartitionSpec as P


def extended_2(cells, sides, width):
    for axis, dim in sides:
        count = lax.axis_size(axis)
        head = lax.slice_in_dim(cells, 0, width, axis=dim)
        tail = lax.slice_in_dim(cells, cells.shape[dim] - width, cells.shape[dim], axis=dim)
        cells = jnp.concatenate(
            [
                lax.ppermute(tail, axis, [(i, (i + 1) % count) for i in range(count)]),
                cells,
                lax.ppermute(head, axis, [((i + 1) % count, i) for i in range(count)]),
            ],
            axis=dim,
        )
    return cells


def passed_along(value, axis, steps):
    count = lax.axis_size(axis)
    pairs = [(source, (source + steps) % count) for source in range(count)]
    return lax.ppermute(value, axis, pairs)


def split_three(values):
    upper = values.astype(jnp.bfloat16)
    rest = values - upper.astype(jnp.float32)
    middle = rest.astype(jnp.bfloat16)
    lower = (rest - middle.astype(jnp.float32)).astype(jnp.bfloat16)
    return (upper, middle, lower)


def exact_product(left, values):
    total = None
    for piece in split_three(values):
        term = jnp.dot(left, piece, preferred_element_type=jnp.float32)
        total = term if total is None else total + term
    return total


def exact_spread(selector, values):
    total = None
    for piece in split_three(values):
        term = lax.dot_general(
            selector, piece, (((0,), (0,)), ((), ())), preferred_element_type=jnp.float32
        )
        total = term if total is None else total + term
    return total


def body(
    state,
    species,
    species_bias,
    edge_index,
    edge_count,
    edge_dist,
    trip_index,
    trip_count,
    trip_cos,
    radial_weight,
    norm_gain,
    w_centre,
    w_neigh,
    w_mix,
    w_out,
):
    size_x, size_y, tile_atoms, chans = state.shape
    edges = edge_index.shape[3]
    trips = trip_index.shape[3]
    kinds = species_bias.shape[0]
    flat = state.reshape(-1, chans)
    onehot = (species.reshape(-1)[:, None] == jnp.arange(kinds, dtype=jnp.int32)[None, :]).astype(
        jnp.float32
    )
    proj_a = jnp.dot(flat, w_centre, preferred_element_type=jnp.float32)
    proj_a = proj_a + jnp.dot(onehot, species_bias, precision=lax.Precision.HIGHEST)
    proj_a = proj_a.reshape(size_x, size_y, tile_atoms, chans)
    extended = extended_2(state, (("gx", 0), ("gy", 1)), 1)
    ext_b = jnp.dot(
        extended.reshape(-1, chans), w_neigh, preferred_element_type=jnp.float32
    ).astype(jnp.bfloat16)
    ext_b = ext_b.reshape(size_x + 2, size_y + 2, tile_atoms, chans)
    tiles = size_x * size_y
    grid_x = jnp.arange(size_x, dtype=jnp.int32)[:, None].reshape(tiles)
    grid_y = jnp.broadcast_to(
        jnp.arange(size_y, dtype=jnp.int32)[None, :], (size_x, size_y)
    ).reshape(tiles)
    valid = jnp.arange(edges, dtype=jnp.int32)[None, None, :] < edge_count[:, :, None]
    weight = jnp.where(
        jnp.arange(trips, dtype=jnp.int32)[None, None, :] < trip_count[:, :, None], trip_cos, 0.0
    )
    items = (
        grid_x,
        grid_y,
        edge_index[:, :, 0, :].reshape(tiles, edges),
        edge_index[:, :, 1, :].reshape(tiles, edges),
        valid.reshape(tiles, edges),
        edge_dist.reshape(tiles, edges),
        trip_index[:, :, 0, :].reshape(tiles, trips),
        trip_index[:, :, 1, :].reshape(tiles, trips),
        weight.reshape(tiles, trips),
    )
    atom_ids = jnp.arange(tile_atoms, dtype=jnp.int32)[None, :]
    nearby_ids = jnp.arange(9 * tile_atoms, dtype=jnp.int32)[None, :]
    zero = jnp.zeros((), jnp.int32)

    def tile_step(agg, item):
        tx, ty, centre_t, code_t, valid_t, dist_t, recv_t, partner_t, weight_t = item
        own_a = lax.dynamic_slice(proj_a, (tx, ty, zero, zero), (1, 1, tile_atoms, chans)).reshape(
            tile_atoms, chans
        )
        nearby = lax.dynamic_slice(ext_b, (tx, ty, zero, zero), (3, 3, tile_atoms, chans)).reshape(
            9 * tile_atoms, chans
        )
        pick_centre = (centre_t[:, None] == atom_ids).astype(jnp.bfloat16)
        pick_near = (code_t[:, None] == nearby_ids).astype(jnp.bfloat16)
        centre_rows = exact_product(pick_centre, own_a)
        near_rows = jnp.dot(pick_near, nearby, preferred_element_type=jnp.float32)
        pre = centre_rows + near_rows + dist_t[:, None] * radial_weight
        envelope = (1.0 - dist_t * dist_t) ** 2
        feat = jnp.where(valid_t[:, None], jax.nn.silu(pre) * envelope[:, None], 0.0).astype(
            jnp.bfloat16
        )
        mixed = jnp.dot(feat, w_mix, preferred_element_type=jnp.float32).astype(jnp.bfloat16)
        links = jnp.zeros((edges, edges), jnp.float32).at[recv_t, partner_t].add(weight_t)
        edge_msg = feat.astype(jnp.float32) * exact_product(links, mixed)
        spread = exact_spread(pick_near, edge_msg).reshape(3, 3, tile_atoms, chans)
        region = lax.dynamic_slice(agg, (tx, ty, zero, zero), (3, 3, tile_atoms, chans)) + spread
        return (lax.dynamic_update_slice(agg, region, (tx, ty, zero, zero)), None)

    agg = jnp.zeros((size_x + 2, size_y + 2, tile_atoms, chans), jnp.float32)
    agg, _ = lax.scan(tile_step, agg, items)
    for step_by in (1, -1):
        outgoing = agg[size_x + 1] if step_by == 1 else agg[0]
        arrived = passed_along(outgoing, "gx", step_by)
        target = 1 if step_by == 1 else size_x
        agg = agg.at[target].add(arrived)
    for step_by in (1, -1):
        outgoing = agg[1 : size_x + 1, size_y + 1] if step_by == 1 else agg[1 : size_x + 1, 0]
        arrived = passed_along(outgoing, "gy", step_by)
        target = 1 if step_by == 1 else size_y
        agg = agg.at[1 : size_x + 1, target].add(arrived)
    owned = agg[1 : size_x + 1, 1 : size_y + 1].reshape(-1, chans)
    scale = lax.rsqrt(jnp.mean(owned * owned, axis=-1, keepdims=True) + 1e-05)
    normed = (owned * scale * norm_gain).astype(jnp.bfloat16)
    updated = flat.astype(jnp.float32) + jnp.dot(normed, w_out, preferred_element_type=jnp.float32)
    return updated.astype(jnp.bfloat16).reshape(size_x, size_y, tile_atoms, chans)


def solution(mesh):
    placed = (
        P("gx", "gy", None, None),
        P("gx", "gy", None),
        P(),
        P("gx", "gy", None, None),
        P("gx", "gy"),
        P("gx", "gy", None),
        P("gx", "gy", None, None),
        P("gx", "gy"),
        P("gx", "gy", None),
        P(),
        P(),
        P(),
        P(),
        P(),
        P(),
    )
    return jax.shard_map(
        body, mesh=mesh, in_specs=placed, out_specs=P("gx", "gy", None, None), check_vma=False
    )
```

profile of v0, /device:TPU:1, one launch (start us, length us, event | category | flops | bytes accessed | tf_op | source)
XLA Modules:
  0.0 121.6 jit_solution(5633178104334854782)
XLA Ops:
  0.0 0.9 fusion.40
  0.9 21.9 %collective-permute-start.1 = (bf16[1,1,128,256]{3,2,1,0:T(8,128)(2,1)S(1)}, bf16[1,1,128,256]{3,2,1,0:T(8,128)(2,1)S(1)}, u32[]{:S(2)}, u32[]{:S(2)}) collective-permute-start(bf16[1,1,128,256]{3,2,1,0:T(8,128)(2,1)S(1)} %get-tuple-element.231), channel_id=1, source_target_pairs={{16,0},{32,16},{48,32},{64,48},{80,64},{96,80},{112,96},{128,112},... | collective-permute-start | bytes 196616 | tf_op jit(solution)/shard_map/ppermute | solution.py:16
  22.8 1.9 %collective-permute-start = (bf16[1,1,128,256]{3,2,1,0:T(8,128)(2,1)S(1)}, bf16[1,1,128,256]{3,2,1,0:T(8,128)(2,1)S(1)}, u32[]{:S(2)}, u32[]{:S(2)}) collective-permute-start(bf16[1,1,128,256]{3,2,1,0:T(8,128)(2,1)S(1)} %get-tuple-element.232), channel_id=1, source_target_pairs={{0,16},{16,32},{32,48},{48,64},{64,80},{80,96},{96,112},{112,128},... | collective-permute-start | bytes 196616 | tf_op jit(solution)/shard_map/ppermute | solution.py:14
  24.7 0.8 fusion.42
  25.5 0.8 fusion.41
  26.3 0.8 fusion.38
  27.1 1.0 fusion.36
  28.1 3.3 %collective-permute-done = bf16[1,1,128,256]{3,2,1,0:T(8,128)(2,1)S(1)} collective-permute-done((bf16[1,1,128,256]{3,2,1,0:T(8,128)(2,1)S(1)}, bf16[1,1,128,256]{3,2,1,0:T(8,128)(2,1)S(1)}, u32[]{:S(2)}, u32[]{:S(2)}) %collective-permute-start) | collective-permute-done | bytes 65568 | tf_op jit(solution)/shard_map/ppermute | solution.py:14
  31.4 0.9 constant_dynamic-update-slice_fusion.1
  32.4 4.0 %collective-permute-start.3 = (bf16[4,1,128,256]{3,2,1,0:T(8,128)(2,1)S(1)}, bf16[4,1,128,256]{3,2,1,0:T(8,128)(2,1)S(1)}, u32[]{:S(2)}, u32[]{:S(2)}) collective-permute-start(bf16[4,1,128,256]{3,2,1,0:T(8,128)(2,1)S(1)} %constant_dynamic-update-slice_fusion), channel_id=1, source_target_pairs={{1,0},{2,1},{3,2},{4,3},{5,4},{6,5},{7,6},{8,7},{9,8},{10,9},{11,1... | collective-permute-start | bytes 786440 | tf_op jit(solution)/shard_map/ppermute | solution.py:16
  36.4 2.2 %collective-permute-start.2 = (bf16[4,1,128,256]{3,2,1,0:T(8,128)(2,1)S(1)}, bf16[4,1,128,256]{3,2,1,0:T(8,128)(2,1)S(1)}, u32[]{:S(2)}, u32[]{:S(2)}) collective-permute-start(bf16[4,1,128,256]{3,2,1,0:T(8,128)(2,1)S(1)} %constant_dynamic-update-slice_fusion), channel_id=1, source_target_pairs={{0,1},{1,2},{2,3},{3,4},{4,5},{5,6},{6,7},{7,8},{8,9},{9,10},{10,1... | collective-permute-start | bytes 786440 | tf_op jit(solution)/shard_map/ppermute | solution.py:14
  38.6 0.7 iota_compare_fusion.17
  39.3 0.7 copy.47
  40.0 1.1 convolution_add_fusion.7
  41.2 2.4 %collective-permute-done.2 = bf16[4,1,128,256]{3,2,1,0:T(8,128)(2,1)S(1)} collective-permute-done((bf16[4,1,128,256]{3,2,1,0:T(8,128)(2,1)S(1)}, bf16[4,1,128,256]{3,2,1,0:T(8,128)(2,1)S(1)}, u32[]{:S(2)}, u32[]{:S(2)}) %collective-permute-start.2) | collective-permute-done | bytes 262176 | tf_op jit(solution)/shard_map/ppermute | solution.py:14
  43.7 0.4 convolution_convert_fusion.1
  44.3 0.3 copy-done.7
  44.6 36.8 %while.15 = (s32[]{:T(128)}, f32[4,3,128,256]{3,2,1,0:T(8,128)S(1)}, s32[2]{0:T(128)S(1)}, s32[2,512]{1,0:T(2,128)S(1)}, pred[2,512]{1,0:T(4,128)(4,1)S(1)}, /*i...) while((s32[]{:T(128)}, ...), condition=%wide.region_2.3_spmd.clone, body=%wide.region_0.2_spmd.clone.sunk | while | flops 1787190784 | bytes 36437556 | solution.py:137
  44.7 0.7 dynamic_slice.100
  49.8 0.7 select_convert_fusion.2
  50.7 0.5 copy-done.1
  51.2 6.2 %scatter_custom_fusion.6 = f32[262144]{0:T(1024)S(1)} fusion(s32[1024]{0:T(1024)S(1)} %broadcast_select_fusion.2, f32[1024]{0:T(1024)S(1)} %bitcast.158, f32[]{:T(128)} %constant.147.clone.1..sunk), kind=kCustom, calls=%fused_computation.21.clone.1 | custom fusion | flops 1024 | bytes 1048580 | tf_op jit(solution)/shard_map/while
  58.0 0.3 convolution_add_fusion.15
  58.3 0.3 copy-done.2
  58.6 0.3 fusion.88
  59.0 0.9 fusion.89
  59.9 0.9 convolution_add_fusion.16
  60.8 0.9 convolution_add_fusion.17
  62.1 0.8 copy-done.4
  63.1 0.7 dynamic_slice.100
  68.2 0.7 select_convert_fusion.2
  69.1 0.5 copy-done.1
  69.6 6.2 %scatter_custom_fusion.6 = f32[262144]{0:T(1024)S(1)} fusion(s32[1024]{0:T(1024)S(1)} %broadcast_select_fusion.2, f32[1024]{0:T(1024)S(1)} %bitcast.158, f32[]{:T(128)} %constant.147.clone.1..sunk), kind=kCustom, calls=%fused_computation.21.clone.1 | custom fusion | flops 1024 | bytes 1048580 | tf_op jit(solution)/shard_map/while
  76.7 0.3 copy-done.2
  77.0 0.3 fusion.88
  77.3 0.9 fusion.89
  78.3 0.9 convolution_add_fusion.16
  79.2 0.9 convolution_add_fusion.17
  80.5 0.8 copy-done.4
  81.4 1.9 %collective-permute-start.4 = (f32[3,128,256]{2,1,0:T(8,128)S(1)}, f32[3,128,256]{2,1,0:T(8,128)S(1)}, u32[]{:S(2)}, u32[]{:S(2)}) collective-permute-start(f32[3,128,256]{2,1,0:T(8,128)S(1)} %slice_bitcast_fusion.1), channel_id=1, source_target_pairs={{0,16},{16,32},{32,48},{48,64},{64,80},{80,96},{96,112},{112,128},... | collective-permute-start | bytes 1179656 | tf_op jit(solution)/shard_map/ppermute | solution.py:26
  83.3 10.7 %collective-permute-done.4 = f32[3,128,256]{2,1,0:T(8,128)S(1)} collective-permute-done((f32[3,128,256]{2,1,0:T(8,128)S(1)}, f32[3,128,256]{2,1,0:T(8,128)S(1)}, u32[]{:S(2)}, u32[]{:S(2)}) %collective-permute-start.4) | collective-permute-done | bytes 393248 | tf_op jit(solution)/shard_map/ppermute | solution.py:26
  94.2 2.1 %collective-permute-start.5 = (f32[3,128,256]{2,1,0:T(8,128)S(1)}, f32[3,128,256]{2,1,0:T(8,128)S(1)}, u32[]{:S(2)}, u32[]{:S(2)}) collective-permute-start(f32[3,128,256]{2,1,0:T(8,128)S(1)} %slice_bitcast_fusion), channel_id=1, source_target_pairs={{0,1008},{16,0},{32,16},{48,32},{64,48},{80,64},{96,80},{112,96},{... | collective-permute-start | bytes 1179656 | tf_op jit(solution)/shard_map/ppermute | solution.py:26
  96.3 6.6 %collective-permute-done.5 = f32[3,128,256]{2,1,0:T(8,128)S(1)} collective-permute-done((f32[3,128,256]{2,1,0:T(8,128)S(1)}, f32[3,128,256]{2,1,0:T(8,128)S(1)}, u32[]{:S(2)}, u32[]{:S(2)}) %collective-permute-start.5) | collective-permute-done | bytes 393248 | tf_op jit(solution)/shard_map/ppermute | solution.py:26
  103.0 8.1 %collective-permute-start.6 = (f32[2,128,256]{2,1,0:T(8,128)S(1)}, f32[2,128,256]{2,1,0:T(8,128)S(1)}, u32[]{:S(2)}, u32[]{:S(2)}) collective-permute-start(f32[2,128,256]{2,1,0:T(8,128)S(1)} %get-tuple-element.229), channel_id=1, source_target_pairs={{0,1},{1,2},{2,3},{3,4},{4,5},{5,6},{6,7},{7,8},{8,9},{9,10},{10,1... | collective-permute-start | bytes 786440 | tf_op jit(solution)/shard_map/ppermute | solution.py:26
  111.2 1.9 %collective-permute-start.7 = (f32[2,128,256]{2,1,0:T(8,128)S(1)}, f32[2,128,256]{2,1,0:T(8,128)S(1)}, u32[]{:S(2)}, u32[]{:S(2)}) collective-permute-start(f32[2,128,256]{2,1,0:T(8,128)S(1)} %get-tuple-element.230), channel_id=1, source_target_pairs={{0,15},{1,0},{2,1},{3,2},{4,3},{5,4},{6,5},{7,6},{8,7},{9,8},{10,9... | collective-permute-start | bytes 786440 | tf_op jit(solution)/shard_map/ppermute | solution.py:26
  113.1 1.4 %collective-permute-done.6 = f32[2,128,256]{2,1,0:T(8,128)S(1)} collective-permute-done((f32[2,128,256]{2,1,0:T(8,128)S(1)}, f32[2,128,256]{2,1,0:T(8,128)S(1)}, u32[]{:S(2)}, u32[]{:S(2)}) %collective-permute-start.6) | collective-permute-done | bytes 262176 | tf_op jit(solution)/shard_map/ppermute | solution.py:26
  114.5 6.0 %collective-permute-done.7 = f32[2,128,256]{2,1,0:T(8,128)S(1)} collective-permute-done((f32[2,128,256]{2,1,0:T(8,128)S(1)}, f32[2,128,256]{2,1,0:T(8,128)S(1)}, u32[]{:S(2)}, u32[]{:S(2)}) %collective-permute-start.7) | collective-permute-done | bytes 262176 | tf_op jit(solution)/shard_map/ppermute | solution.py:26
  120.8 0.8 fusion.29
  (151 shorter events, 5.7 us)
Async XLA Ops:
  0.0 43.7 %copy-start = (bf16[256,256]{1,0:T(8,128)(2,1)S(1)}, bf16[256,256]{1,0:T(8,128)(2,1)}, u32[]{:S(2)}) copy-start(bf16[256,256]{1,0:T(8,128)(2,1)} %param.37) | copy-start | bytes 393220
  0.9 31.4 %collective-permute-start.1 = (bf16[1,1,128,256]{3,2,1,0:T(8,128)(2,1)S(1)}, bf16[1,1,128,256]{3,2,1,0:T(8,128)(2,1)S(1)}, u32[]{:S(2)}, u32[]{:S(2)}) collective-permute-start(bf16[1,1,128,256]{3,2,1,0:T(8,128)(2,1)S(1)} %get-tuple-element.231), channel_id=1, source_target_pairs={{16,0},{32,16},{48,32},{64,48},{80,64},{96,80},{112,96},{128,112},... | collective-permute-start | bytes 196616 | tf_op jit(solution)/shard_map/ppermute | solution.py:16
  22.8 8.6 %collective-permute-start = (bf16[1,1,128,256]{3,2,1,0:T(8,128)(2,1)S(1)}, bf16[1,1,128,256]{3,2,1,0:T(8,128)(2,1)S(1)}, u32[]{:S(2)}, u32[]{:S(2)}) collective-permute-start(bf16[1,1,128,256]{3,2,1,0:T(8,128)(2,1)S(1)} %get-tuple-element.232), channel_id=1, source_target_pairs={{0,16},{16,32},{32,48},{48,64},{64,80},{80,96},{96,112},{112,128},... | collective-permute-start | bytes 196616 | tf_op jit(solution)/shard_map/ppermute | solution.py:14
  32.4 8.8 %collective-permute-start.3 = (bf16[4,1,128,256]{3,2,1,0:T(8,128)(2,1)S(1)}, bf16[4,1,128,256]{3,2,1,0:T(8,128)(2,1)S(1)}, u32[]{:S(2)}, u32[]{:S(2)}) collective-permute-start(bf16[4,1,128,256]{3,2,1,0:T(8,128)(2,1)S(1)} %constant_dynamic-update-slice_fusion), channel_id=1, source_target_pairs={{1,0},{2,1},{3,2},{4,3},{5,4},{6,5},{7,6},{8,7},{9,8},{10,9},{11,1... | collective-permute-start | bytes 786440 | tf_op jit(solution)/shard_map/ppermute | solution.py:16
  36.4 7.2 %collective-permute-start.2 = (bf16[4,1,128,256]{3,2,1,0:T(8,128)(2,1)S(1)}, bf16[4,1,128,256]{3,2,1,0:T(8,128)(2,1)S(1)}, u32[]{:S(2)}, u32[]{:S(2)}) collective-permute-start(bf16[4,1,128,256]{3,2,1,0:T(8,128)(2,1)S(1)} %constant_dynamic-update-slice_fusion), channel_id=1, source_target_pairs={{0,1},{1,2},{2,3},{3,4},{4,5},{5,6},{6,7},{7,8},{8,9},{9,10},{10,1... | collective-permute-start | bytes 786440 | tf_op jit(solution)/shard_map/ppermute | solution.py:14
  44.6 4.0 %copy-start.28 = (s32[2]{0:T(128)}, s32[2]{0:T(128)S(1)}, u32[]{:S(2)}) copy-start(s32[2]{0:T(128)S(1)} %get-tuple-element.376) | copy-start | bytes 28 | tf_op jit(solution)/shard_map/while
  44.6 4.0 %copy-start.21 = (f32[2,512]{1,0:T(2,128)}, f32[2,512]{1,0:T(2,128)S(1)}, u32[]{:S(2)}) copy-start(f32[2,512]{1,0:T(2,128)S(1)} %get-tuple-element.382) | copy-start | bytes 12292 | tf_op jit(solution)/shard_map/while
  44.6 4.0 %copy-start.11 = (f32[2,1024]{1,0:T(2,128)}, f32[2,1024]{1,0:T(2,128)S(1)}, u32[]{:S(2)}) copy-start(f32[2,1024]{1,0:T(2,128)S(1)} %get-tuple-element.386) | copy-start | bytes 24580 | tf_op jit(solution)/shard_map/while
  44.6 4.1 %copy-start.13 = (s32[2,1024]{1,0:T(2,128)}, s32[2,1024]{1,0:T(2,128)S(1)}, u32[]{:S(2)}) copy-start(s32[2,1024]{1,0:T(2,128)S(1)} %get-tuple-element.385) | copy-start | bytes 24580 | tf_op jit(solution)/shard_map/while
  44.6 4.1 %copy-start.17 = (s32[2,512]{1,0:T(2,128)}, s32[2,512]{1,0:T(2,128)S(1)}, u32[]{:S(2)}) copy-start(s32[2,512]{1,0:T(2,128)S(1)} %get-tuple-element.379) | copy-start | bytes 12292 | tf_op jit(solution)/shard_map/while
  44.7 5.1 %copy-start.3 = (bf16[4,3,128,256]{3,2,1,0:T(8,128)(2,1)}, bf16[4,3,128,256]{3,2,1,0:T(8,128)(2,1)S(1)}, u32[]{:S(2)}) copy-start(bf16[4,3,128,256]{3,2,1,0:T(8,128)(2,1)S(1)} %get-tuple-element.381) | copy-start | bytes 2359300 | tf_op jit(solution)/shard_map/while
  44.7 5.1 %copy-start.15 = (s32[2,1024]{1,0:T(2,128)}, s32[2,1024]{1,0:T(2,128)S(1)}, u32[]{:S(2)}) copy-start(s32[2,1024]{1,0:T(2,128)S(1)} %get-tuple-element.384) | copy-start | bytes 24580 | tf_op jit(solution)/shard_map/while
  44.7 5.1 %copy-start.19 = (s32[2,512]{1,0:T(2,128)}, s32[2,512]{1,0:T(2,128)S(1)}, u32[]{:S(2)}) copy-start(s32[2,512]{1,0:T(2,128)S(1)} %get-tuple-element.377) | copy-start | bytes 12292 | tf_op jit(solution)/shard_map/while
  44.7 5.8 %copy-start.5 = (f32[2,1,128,256]{3,2,1,0:T(8,128)}, f32[2,1,128,256]{3,2,1,0:T(8,128)S(1)}, u32[]{:S(2)}) copy-start(f32[2,1,128,256]{3,2,1,0:T(8,128)S(1)} %get-tuple-element.380) | copy-start | bytes 786436 | tf_op jit(solution)/shard_map/while
  61.7 1.2 copy-start.6
  61.7 1.2 copy-start.8
  61.7 1.2 copy-start.12
  61.7 1.2 copy-start.14
  61.8 1.2 copy-start.16
  61.8 1.2 copy-start.18
  61.8 1.2 copy-start.20
  61.8 1.2 copy-start.22
  61.8 1.2 copy-start.24
  63.0 4.0 %copy-start.28 = (s32[2]{0:T(128)}, s32[2]{0:T(128)S(1)}, u32[]{:S(2)}) copy-start(s32[2]{0:T(128)S(1)} %get-tuple-element.376) | copy-start | bytes 28 | tf_op jit(solution)/shard_map/while
  63.0 4.0 %copy-start.21 = (f32[2,512]{1,0:T(2,128)}, f32[2,512]{1,0:T(2,128)S(1)}, u32[]{:S(2)}) copy-start(f32[2,512]{1,0:T(2,128)S(1)} %get-tuple-element.382) | copy-start | bytes 12292 | tf_op jit(solution)/shard_map/while
  63.0 4.0 %copy-start.11 = (f32[2,1024]{1,0:T(2,128)}, f32[2,1024]{1,0:T(2,128)S(1)}, u32[]{:S(2)}) copy-start(f32[2,1024]{1,0:T(2,128)S(1)} %get-tuple-element.386) | copy-start | bytes 24580 | tf_op jit(solution)/shard_map/while
  63.0 4.1 %copy-start.13 = (s32[2,1024]{1,0:T(2,128)}, s32[2,1024]{1,0:T(2,128)S(1)}, u32[]{:S(2)}) copy-start(s32[2,1024]{1,0:T(2,128)S(1)} %get-tuple-element.385) | copy-start | bytes 24580 | tf_op jit(solution)/shard_map/while
  63.0 4.1 %copy-start.17 = (s32[2,512]{1,0:T(2,128)}, s32[2,512]{1,0:T(2,128)S(1)}, u32[]{:S(2)}) copy-start(s32[2,512]{1,0:T(2,128)S(1)} %get-tuple-element.379) | copy-start | bytes 12292 | tf_op jit(solution)/shard_map/while
  63.0 5.1 %copy-start.3 = (bf16[4,3,128,256]{3,2,1,0:T(8,128)(2,1)}, bf16[4,3,128,256]{3,2,1,0:T(8,128)(2,1)S(1)}, u32[]{:S(2)}) copy-start(bf16[4,3,128,256]{3,2,1,0:T(8,128)(2,1)S(1)} %get-tuple-element.381) | copy-start | bytes 2359300 | tf_op jit(solution)/shard_map/while
  63.1 5.1 %copy-start.15 = (s32[2,1024]{1,0:T(2,128)}, s32[2,1024]{1,0:T(2,128)S(1)}, u32[]{:S(2)}) copy-start(s32[2,1024]{1,0:T(2,128)S(1)} %get-tuple-element.384) | copy-start | bytes 24580 | tf_op jit(solution)/shard_map/while
  63.1 5.1 %copy-start.19 = (s32[2,512]{1,0:T(2,128)}, s32[2,512]{1,0:T(2,128)S(1)}, u32[]{:S(2)}) copy-start(s32[2,512]{1,0:T(2,128)S(1)} %get-tuple-element.377) | copy-start | bytes 12292 | tf_op jit(solution)/shard_map/while
  63.1 5.8 %copy-start.5 = (f32[2,1,128,256]{3,2,1,0:T(8,128)}, f32[2,1,128,256]{3,2,1,0:T(8,128)S(1)}, u32[]{:S(2)}) copy-start(f32[2,1,128,256]{3,2,1,0:T(8,128)S(1)} %get-tuple-element.380) | copy-start | bytes 786436 | tf_op jit(solution)/shard_map/while
  80.1 1.2 copy-start.6
  80.1 1.2 copy-start.8
  80.1 1.2 copy-start.12
  80.1 1.2 copy-start.14
  80.1 1.2 copy-start.16
  80.2 1.2 copy-start.18
  80.2 1.2 copy-start.20
  80.2 1.2 copy-start.22
  80.2 1.2 copy-start.24
  81.4 12.7 %collective-permute-start.4 = (f32[3,128,256]{2,1,0:T(8,128)S(1)}, f32[3,128,256]{2,1,0:T(8,128)S(1)}, u32[]{:S(2)}, u32[]{:S(2)}) collective-permute-start(f32[3,128,256]{2,1,0:T(8,128)S(1)} %slice_bitcast_fusion.1), channel_id=1, source_target_pairs={{0,16},{16,32},{32,48},{48,64},{64,80},{80,96},{96,112},{112,128},... | collective-permute-start | bytes 1179656 | tf_op jit(solution)/shard_map/ppermute | solution.py:26
  94.2 26.4 %copy-start.25 = (f32[256]{0:T(256)S(1)}, f32[256]{0:T(256)}, u32[]{:S(2)}) copy-start(f32[256]{0:T(256)} %param.35) | copy-start | bytes 3076
  94.2 26.5 %copy-start.9 = (bf16[2,1,128,256]{3,2,1,0:T(8,128)(2,1)S(1)}, bf16[2,1,128,256]{3,2,1,0:T(8,128)(2,1)}, u32[]{:S(2)}) copy-start(bf16[2,1,128,256]{3,2,1,0:T(8,128)(2,1)} %param.25) | copy-start | bytes 393220
  94.2 26.5 %copy-start.10 = (bf16[256,256]{1,0:T(8,128)(2,1)S(1)}, bf16[256,256]{1,0:T(8,128)(2,1)}, u32[]{:S(2)}) copy-start(bf16[256,256]{1,0:T(8,128)(2,1)} %param.39) | copy-start | bytes 393220
  94.2 8.7 %collective-permute-start.5 = (f32[3,128,256]{2,1,0:T(8,128)S(1)}, f32[3,128,256]{2,1,0:T(8,128)S(1)}, u32[]{:S(2)}, u32[]{:S(2)}) collective-permute-start(f32[3,128,256]{2,1,0:T(8,128)S(1)} %slice_bitcast_fusion), channel_id=1, source_target_pairs={{0,1008},{16,0},{32,16},{48,32},{64,48},{80,64},{96,80},{112,96},{... | collective-permute-start | bytes 1179656 | tf_op jit(solution)/shard_map/ppermute | solution.py:26
  103.0 11.4 %collective-permute-start.6 = (f32[2,128,256]{2,1,0:T(8,128)S(1)}, f32[2,128,256]{2,1,0:T(8,128)S(1)}, u32[]{:S(2)}, u32[]{:S(2)}) collective-permute-start(f32[2,128,256]{2,1,0:T(8,128)S(1)} %get-tuple-element.229), channel_id=1, source_target_pairs={{0,1},{1,2},{2,3},{3,4},{4,5},{5,6},{6,7},{7,8},{8,9},{9,10},{10,1... | collective-permute-start | bytes 786440 | tf_op jit(solution)/shard_map/ppermute | solution.py:26
  111.2 9.3 %collective-permute-start.7 = (f32[2,128,256]{2,1,0:T(8,128)S(1)}, f32[2,128,256]{2,1,0:T(8,128)S(1)}, u32[]{:S(2)}, u32[]{:S(2)}) collective-permute-start(f32[2,128,256]{2,1,0:T(8,128)S(1)} %get-tuple-element.230), channel_id=1, source_target_pairs={{0,15},{1,0},{2,1},{3,2},{4,3},{5,4},{6,5},{7,6},{8,7},{9,8},{10,9... | collective-permute-start | bytes 786440 | tf_op jit(solution)/shard_map/ppermute | solution.py:26
  (13 other events, 12.9 us)
where the time goes:
time: 123 us; the launch traced here: 122 us
  starting transfers between devices  44 us (36%)
  waiting for transfers between devices  30.4 us (25%)
  other arithmetic  15.1 us (12%)
  matrix products  14.1 us (11%)
  local copies, waits for them, and re-layouts  10.4 us (8%)
  loops' own time  7.26 us (6%)
    ppermute x2, starting transfers between devices, extended_2(): lax.ppermute(head, axis, [((i + 1) % count, i) for i in range(count)])  25.9 us
    ppermute x4, waiting for transfers between devices, passed_along(): return lax.ppermute(value, axis, pairs)  24.7 us
    ppermute x4, starting transfers between devices, passed_along(): return lax.ppermute(value, axis, pairs)  14 us
    while x8, other arithmetic  12.6 us
    another operation x1, loops' own time, body(): agg, _ = lax.scan(tile_step, agg, items)  7.26 us
    ppermute x2, waiting for transfers between devices, extended_2(): lax.ppermute(tail, axis, [(i, (i + 1) % count) for i in range(count)])  5.7 us
    dot_general x6, matrix products, exact_spread(): lax.dot_general(selector, piece, (((0,), (0,)), ((), ())), preferred_elem...  5.45 us
    ppermute x2, starting transfers between devices, extended_2(): lax.ppermute(tail, axis, [(i, (i + 1) % count) for i in range(count)])  4.12 us
  transfers between devices with their start and end apart: 8, of which 6 were waited for; matrix products, arithmetic and copies ran while one was open for 6% of the time, Pallas kernels for 0%

commit v1 on v0

v1 whole, which is shorter than its diff:
```python
import jax
import jax.numpy as jnp
from jax import lax
from jax.experimental import pallas as pl
from jax.experimental.pallas import tpu as pltpu
from jax.sharding import PartitionSpec as P


F32 = jnp.float32
BF16 = jnp.bfloat16
NT = (((1,), (1,)), ((), ()))
TN = (((0,), (0,)), ((), ()))
VMEM_LIMIT = 32 * 1024 * 1024


def core_bit():
    return lax.rem(lax.axis_index("gy"), 2)


def dot(left, right, dims=(((1,), (0,)), ((), ()))):
    return lax.dot_general(left, right, dims, preferred_element_type=F32)


def onehot(index, first, count):
    rows = lax.broadcasted_iota(jnp.int32, (count, index.shape[1]), 0) + first
    return jnp.where(rows == index, 1.0, 0.0).astype(BF16)


def near_codes(pack_ref, holder, core, edges, atoms):
    code = pack_ref[holder, core, 3:4, edges : 2 * edges].astype(jnp.int32)
    slot = jnp.bitwise_and(code, atoms - 1)
    return jnp.where(core == 1, 8 * atoms + 2 * slot - code, code)


def pack_kernel(count_e, count_t, index_e, dist, index_t, cosine, species, out):
    edges = dist.shape[2]
    trips = cosine.shape[2]
    atoms = species.shape[2]
    out[...] = jnp.zeros(out.shape, F32)
    lanes_e = lax.broadcasted_iota(jnp.int32, (1, edges), 1)
    lanes_t = lax.broadcasted_iota(jnp.int32, (1, trips), 1)
    for row in range(2):
        out[row, 0:2, :] = index_t[row, 0].astype(F32)
        out[row, 2:3, :] = jnp.where(lanes_t < count_t[row, 0], cosine[row], 0.0)
        out[row, 3:4, 0:edges] = index_e[row, 0, 0:1, :].astype(F32)
        out[row, 3:4, edges : 2 * edges] = index_e[row, 0, 1:2, :].astype(F32)
        reach = dist[row]
        envelope = (1.0 - reach * reach) ** 2
        out[row, 4:5, 0:edges] = reach
        out[row, 4:5, edges : 2 * edges] = jnp.where(lanes_e < count_e[row, 0], envelope, 0.0)
        out[row, 5:6, 0:atoms] = species[row].astype(F32)


def prep_kernel(
    pack, own, edge_col, pair_own, pair_edge, w_neigh, w_centre, bias, radial, links, pre, rows128
):
    core = core_bit()
    far = 1 - core
    edges = links.shape[1]
    trips = pack.shape[3]
    atoms = own.shape[2]
    kinds = bias.shape[0]
    for tile in range(2):
        holder = core if tile == 0 else far
        recv = pack[holder, core, 0:1, :].astype(jnp.int32)
        partner = pack[holder, core, 1:2, :].astype(jnp.int32)
        weight = pack[holder, core, 2:3, :]
        into = onehot(recv, 0, edges)
        rows = lax.broadcasted_iota(jnp.int32, (edges, trips), 0)
        out_of = jnp.where(rows == partner, weight, 0.0).astype(BF16)
        links[tile] = dot(out_of, into, NT).astype(BF16)
    rows128[...] = jnp.zeros(rows128.shape, F32)
    rows128[0:kinds, :] = bias[...]
    rows128[kinds : kinds + 1, :] = radial[...]
    columns = jnp.transpose(rows128[...])
    neigh_t = jnp.transpose(w_neigh[...])
    centre_t = jnp.transpose(w_centre[...])

    def row_states(row):
        return [edge_col[row, 0], own[row, 0], pair_own[far, row, 0], pair_edge[far, row, 0]]

    mine = row_states(core)
    other = row_states(far)
    near = []
    for states in (mine, other):
        stacked = jnp.concatenate(states, axis=0)
        near.append(dot(neigh_t, stacked, NT).astype(BF16))
    for tile in range(2):
        holder = core if tile == 0 else far
        kind = pack[holder, core, 5:6, 0:atoms]
        proj = dot(centre_t, mine[1 + tile], NT)
        for s in range(kinds):
            proj = proj + jnp.where(kind == float(s), columns[:, s : s + 1], 0.0)
        upper = proj.astype(BF16)
        lower = (proj - upper.astype(F32)).astype(BF16)
        span = slice(tile * atoms, (tile + 3) * atoms)
        values = jnp.concatenate([near[0][:, span], near[1][:, span], upper, lower], axis=1)
        code = near_codes(pack, holder, core, edges, atoms)
        centre = pack[holder, core, 3:4, 0:edges].astype(jnp.int32)
        pick_centre = onehot(centre, 0, atoms)
        picks = jnp.concatenate(
            [onehot(code, 3 * atoms, 6 * atoms), pick_centre, pick_centre], axis=0
        )
        reach = pack[holder, core, 4:5, 0:edges]
        pre[tile] = dot(values, picks) + columns[:, kinds : kinds + 1] * reach


def edge_kernel(
    pack,
    links,
    pre,
    remote_own,
    remote_edge,
    w_neigh,
    w_mix,
    post,
    side,
    owned,
    remote_out,
    corner_near,
    corner_far,
):
    core = core_bit()
    far = 1 - core
    edges = links.shape[1]
    atoms = remote_own.shape[1]
    neigh_t = jnp.transpose(w_neigh[...])
    mix_t = jnp.transpose(w_mix[...])
    stacked = jnp.concatenate(
        [remote_edge[core], remote_own[core], remote_own[far], remote_edge[far]], axis=0
    )
    near = dot(neigh_t, stacked, NT).astype(BF16)
    spreads = []
    for tile in range(2):
        holder = core if tile == 0 else far
        code = near_codes(pack, holder, core, edges, atoms)
        envelope = pack[holder, core, 4:5, edges : 2 * edges]
        pick = onehot(code, 0, 9 * atoms)
        total = pre[tile] + dot(near[:, tile * atoms : (tile + 3) * atoms], pick[0 : 3 * atoms])
        feat = (0.5 * total * (1.0 + jnp.tanh(0.5 * total)) * envelope).astype(BF16)
        mixed = dot(mix_t, feat).astype(BF16)
        message = (feat.astype(F32) * dot(mixed, links[tile])).astype(BF16)
        spreads.append(dot(pick, message, NT))

    def cell(row, slot):
        total = None
        for tile in range(2):
            if 0 <= slot - tile < 3:
                at = (3 * row + slot - tile) * atoms
                part = spreads[tile][at : at + atoms]
                total = part if total is None else total + part
        return total

    corner_near[...] = cell(0, 0).astype(BF16)
    corner_far[...] = cell(0, 3).astype(BF16)
    remote_out[core] = cell(0, 1).astype(BF16)
    remote_out[far] = cell(0, 2).astype(BF16)
    for row, at in ((1, core), (2, far)):
        side[at] = cell(row, 0).astype(BF16)
        owned[at] = cell(row, 1)
        post[0, at] = cell(row, 2).astype(BF16)
        post[1, at] = cell(row, 3).astype(BF16)


def side_kernel(side, posts, out):
    far = 1 - core_bit()
    out[...] = (side[...].astype(F32) + posts[far, 1].astype(F32)).astype(BF16)


def final_kernel(
    state, owned, posts, remote, remotes, corner_near, corner_far, side, gain, w_out, out
):
    core = core_bit()
    far = 1 - core
    for row, extra, corner in (
        (core, remote[core], corner_near[...]),
        (far, remotes[far, core], corner_far[...]),
    ):
        total = owned[row] + posts[far, 0, row].astype(F32) + side[row].astype(F32)
        total = total + extra.astype(F32) + corner.astype(F32)
        scale = lax.rsqrt(jnp.mean(total * total, axis=-1, keepdims=True) + 1e-05)
        normed = (total * scale * gain[...]).astype(BF16)
        out[row, 0] = (state[row, 0].astype(F32) + dot(normed, w_out[...])).astype(BF16)


VMEM = pl.BlockSpec(memory_space=pltpu.VMEM)
SMEM = pl.BlockSpec(memory_space=pltpu.SMEM)


def call(kernel, outs, *operands, scratch=(), scalars=0):
    return pl.pallas_call(
        kernel,
        out_shape=outs,
        in_specs=[SMEM] * scalars + [VMEM] * (len(operands) - scalars),
        out_specs=jax.tree.map(lambda _: VMEM, outs),
        scratch_shapes=list(scratch),
        compiler_params=pltpu.CompilerParams(vmem_limit_bytes=VMEM_LIMIT),
    )(*operands)


def pairings():
    count_x, count_y = lax.axis_size("gx"), lax.axis_size("gy")

    def at(x, y):
        return (x % count_x) * count_y + y % count_y

    along_y = []
    along_x, near, far = [], [], []
    for y in range(0, count_y, 2):
        first, second = (y + 2) % count_y, y + 1
        along_y += [(first, second), (second, first)]
    for x in range(count_x):
        for y in range(0, count_y, 2):
            first, second = at(x + 1, y), at(x, y + 1)
            along_x += [(first, second), (second, first)]
            first, second = at(x + 1, y + 2), at(x, y + 1)
            near += [(first, second), (second, first)]
            far += [(at(x, y), at(x - 1, y + 2)), (at(x, y + 1), at(x + 1, y - 1))]
    chips = [[y, y + 1] for y in range(0, count_y, 2)]
    return along_y, along_x, near, far, chips


def body(
    state,
    species,
    species_bias,
    edge_index,
    edge_count,
    edge_dist,
    trip_index,
    trip_count,
    trip_cos,
    radial_weight,
    norm_gain,
    w_centre,
    w_neigh,
    w_mix,
    w_out,
):
    size_x, _, atoms, chans = state.shape
    edges = edge_index.shape[3]
    trips = trip_index.shape[3]
    along_y, along_x, near, far, chips = pairings()
    both = ("gx", "gy")
    core = core_bit()

    def gathered(value):
        return lax.all_gather(value, "gy", axis_index_groups=chips)

    def shaped(*shape, dtype=BF16):
        return jax.ShapeDtypeStruct(shape, dtype)

    def worked_row(pair):
        return lax.dynamic_index_in_dim(pair, core, axis=1, keepdims=False)[:, 0]

    edge_col = lax.ppermute(state, "gy", along_y)
    pair_own = gathered(state)
    remote_own = lax.ppermute(worked_row(pair_own), both, along_x)
    pair_edge = gathered(edge_col)
    remote_edge = lax.ppermute(worked_row(pair_edge), both, along_x)
    packed = call(
        pack_kernel,
        shaped(size_x, 8, trips, dtype=F32),
        edge_count,
        trip_count,
        edge_index,
        edge_dist,
        trip_index,
        trip_cos,
        species,
        scalars=2,
    )
    pack = gathered(packed)
    links, pre = call(
        prep_kernel,
        (shaped(2, edges, edges), shaped(2, chans, edges, dtype=F32)),
        pack,
        state,
        edge_col,
        pair_own,
        pair_edge,
        w_neigh,
        w_centre,
        species_bias,
        radial_weight.reshape(1, chans),
        scratch=[pltpu.VMEM((128, chans), F32)],
    )
    tile = (atoms, chans)
    post, side, owned, remote_out, corner_near, corner_far = call(
        edge_kernel,
        (
            shaped(2, 2, *tile),
            shaped(2, *tile),
            shaped(2, *tile, dtype=F32),
            shaped(2, *tile),
            shaped(*tile),
            shaped(*tile),
        ),
        pack,
        links,
        pre,
        remote_own,
        remote_edge,
        w_neigh,
        w_mix,
    )
    posts = gathered(post)
    side_in = lax.ppermute(call(side_kernel, shaped(2, *tile), side, posts), "gy", along_y)
    remote_in = lax.ppermute(remote_out, both, along_x)
    near_in = lax.ppermute(corner_near, both, near)
    far_in = lax.ppermute(corner_far, both, far)
    remotes = gathered(remote_in)
    return call(
        final_kernel,
        shaped(*state.shape),
        state,
        owned,
        posts,
        remote_in,
        remotes,
        near_in,
        far_in,
        side_in,
        norm_gain.reshape(1, chans),
        w_out,
    )


def solution(mesh):
    placed = (
        P("gx", "gy", None, None),
        P("gx", "gy", None),
        P(),
        P("gx", "gy", None, None),
        P("gx", "gy"),
        P("gx", "gy", None),
        P("gx", "gy", None, None),
        P("gx", "gy"),
        P("gx", "gy", None),
        P(),
        P(),
        P(),
        P(),
        P(),
        P(),
    )
    return jax.shard_map(
        body, mesh=mesh, in_specs=placed, out_specs=P("gx", "gy", None, None), check_vma=False
    )
```

time: 123 us -> 68.6 us (0.56)
  the two profiles are of different devices: /device:TPU:1 before, /device:TPU:32 now
where the time goes in v1:
time: 68.6 us; the launch traced here: 68.2 us
  starting transfers between devices  44.5 us (65%)
  blocking collectives  10.3 us (15%)
  Pallas kernels  5.82 us (8%)
  waiting for transfers between devices  5.25 us (8%)
  local copies, waits for them, and re-layouts  2.17 us (3%)
    ppermute x1, starting transfers between devices, body(): remote_edge = lax.ppermute(worked_row(pair_edge), both, along_x)  11.4 us
    ppermute x1, starting transfers between devices, body(): remote_own = lax.ppermute(worked_row(pair_own), both, along_x)  11.2 us
    all_gather x5, blocking collectives, gathered(): return lax.all_gather(value, 'gy', axis_index_groups=chips)  10.3 us
    ppermute x1, starting transfers between devices, body(): near_in = lax.ppermute(corner_near, both, near)  8.88 us
    pallas_call x5, Pallas kernels, call(): pl.pallas_call(kernel, out_shape=outs, in_specs=[SMEM] * scalars + [VMEM]...  5.82 us
    ppermute x1, waiting for transfers between devices, body(): far_in = lax.ppermute(corner_far, both, far)  5.23 us
    ppermute x1, starting transfers between devices, body(): edge_col = lax.ppermute(state, 'gy', along_y)  5.11 us
    ppermute x1, starting transfers between devices, body(): lax.ppermute(call(side_kernel, shaped(2, *tile), side, posts), 'gy', alon...  3.08 us
  transfers between devices with their start and end apart: 7, of which 1 were waited for; matrix products, arithmetic and copies ran while one was open for 0% of the time, Pallas kernels for 4%

profile of v1, /device:TPU:32, one launch (start us, length us, event | category | flops | bytes accessed | tf_op | source)
XLA Modules:
  0.0 68.2 jit_solution(14782543390465921246)
XLA Ops:
  0.0 5.1 %collective-permute-start = (bf16[2,1,128,256]{3,2,1,0:T(8,128)(2,1)}, bf16[2,1,128,256]{3,2,1,0:T(8,128)(2,1)S(1)}, u32[]{:S(2)}, u32[]{:S(2)}) collective-permute-start(bf16[2,1,128,256]{3,2,1,0:T(8,128)(2,1)} %state.1), channel_id=1, source_target_pairs={{2,1},{1,2},{4,3},{3,4},{6,5},{5,6},{8,7},{7,8},{10,9},{9,10},{12,... | collective-permute-start | bytes 393224 | tf_op jit(solution)/shard_map/ppermute | solution.py:256
  5.1 2.2 %all-gather.1 = bf16[4,1,128,256]{3,2,1,0:T(8,128)(2,1)S(1)} all-gather(bf16[2,1,128,256]{3,2,1,0:T(8,128)(2,1)} %state.1), channel_id=3, replica_groups={{0,1},{2,3},{4,5},{6,7},{8,9},{10,11},{12,13},{14,15},{16,17},{18,19},{..., dimensions={0}, use_global_device_ids=true | all-gather | bytes 393216 | tf_op jit(solution)/shard_map/all_gather | solution.py:248
  7.3 11.2 %collective-permute-start.1 = (bf16[2,128,256]{2,1,0:T(8,128)(2,1)S(1)}, bf16[2,128,256]{2,1,0:T(8,128)(2,1)S(1)}, u32[]{:S(2)}, u32[]{:S(2)}) collective-permute-start(bf16[2,128,256]{2,1,0:T(8,128)(2,1)S(1)} %dynamic-slice_bitcast_fusion.1), channel_id=1, source_target_pairs={{16,1},{1,16},{18,3},{3,18},{20,5},{5,20},{22,7},{7,22},{24,9},{9,... | collective-permute-start | bytes 393224 | tf_op jit(solution)/shard_map/ppermute | solution.py:258
  18.6 0.0 collective-permute-done.edge_col
  18.6 2.0 %all-gather.2 = bf16[4,1,128,256]{3,2,1,0:T(8,128)(2,1)S(1)} all-gather(bf16[2,1,128,256]{3,2,1,0:T(8,128)(2,1)S(1)} %collective-permute-done.edge_col), channel_id=4, replica_groups={{0,1},{2,3},{4,5},{6,7},{8,9},{10,11},{12,13},{14,15},{16,17},{18,19},{..., dimensions={0}, use_global_device_ids=true | all-gather | bytes 393216 | tf_op jit(solution)/shard_map/all_gather | solution.py:248
  20.6 0.0 copy-start.13
  20.6 0.0 copy-start.5
  20.6 0.0 copy-start.6
  20.6 0.0 copy-start.9
  20.6 0.0 copy-start.3
  20.6 0.0 copy-start.14
  20.6 11.4 %collective-permute-start.2 = (bf16[2,128,256]{2,1,0:T(8,128)(2,1)S(1)}, bf16[2,128,256]{2,1,0:T(8,128)(2,1)S(1)}, u32[]{:S(2)}, u32[]{:S(2)}) collective-permute-start(bf16[2,128,256]{2,1,0:T(8,128)(2,1)S(1)} %dynamic-slice_bitcast_fusion), channel_id=1, source_target_pairs={{16,1},{1,16},{18,3},{3,18},{20,5},{5,20},{22,7},{7,22},{24,9},{9,... | collective-permute-start | bytes 393224 | tf_op jit(solution)/shard_map/ppermute | solution.py:260
  32.1 0.0 copy-done.13
  32.1 0.1 copy.18.count_e
  32.2 0.0 copy-done.14
  32.2 0.1 copy.19.count_t
  32.3 0.0 copy-done.5
  32.3 0.0 copy-done.6
  32.3 0.0 copy-done.7
  32.3 0.0 copy-done.9
  32.3 0.6 copy-done.10
  32.9 0.6 shard_map.145
  33.5 0.0 copy-start.8
  33.5 1.9 %all-gather = f32[4,8,1024]{2,1,0:T(8,128)S(1)} all-gather(f32[2,8,1024]{2,1,0:T(8,128)S(1)} %shard_map.145), channel_id=2, replica_groups={{0,1},{2,3},{4,5},{6,7},{8,9},{10,11},{12,13},{14,15},{16,17},{18,19},{..., dimensions={0}, use_global_device_ids=true | all-gather | bytes 196608 | tf_op jit(solution)/shard_map/all_gather | solution.py:248
  35.4 0.0 copy-done.3
  35.4 0.0 copy-done
  35.4 0.0 copy-done.1
  35.4 0.0 copy-done.8
  35.4 0.7 copy-done.12
  36.1 2.1 %shard_map.146 = (bf16[2,512,512]{2,1,0:T(8,128)(2,1)S(1)}, f32[2,256,512]{2,1,0:T(8,128)S(1)}) custom-call(f32[2,2,8,1024]{3,2,1,0:T(8,128)S(1)} %bitcast.17, bf16[2,1,128,256]{3,2,1,0:T(8,128)(2,1)S(1)} %copy-done, bf16[2,1,128,256]{3,2,1,0:T(8,128)(2,1)S(1)} %collective-permute-done.edge_col, bf16[2,2,1,128,256]{4,3,2,1,0:T(8,128)(2,1)S(1)} %bitcast.14, ...), custom_call_target="tpu_custom_call" | custom-call | tf_op jit(solution)/shard_map/pallas_call | solution.py:191
  38.2 0.0 collective-permute-done.1.remote_own
  38.2 0.0 collective-permute-done.2.remote_edge
  38.2 0.0 copy-done.4
  38.2 2.1 %shard_map.147 = (bf16[2,2,128,256]{3,2,1,0:T(8,128)(2,1)S(1)}, bf16[2,128,256]{2,1,0:T(8,128)(2,1)S(1)}, f32[2,128,256]{2,1,0:T(8,128)S(1)}, bf16[2,128,256]{2,...) custom-call(f32[2,2,8,1024]{3,2,1,0:T(8,128)S(1)} %bitcast.18, ...), custom_call_target="tpu_custom_call" | custom-call | tf_op jit(solution)/shard_map/pallas_call | solution.py:191
  40.4 2.7 %collective-permute-start.3 = (bf16[2,128,256]{2,1,0:T(8,128)(2,1)S(1)}, bf16[2,128,256]{2,1,0:T(8,128)(2,1)S(1)}, u32[]{:S(2)}, u32[]{:S(2)}) collective-permute-start(bf16[2,128,256]{2,1,0:T(8,128)(2,1)S(1)} %get-tuple-element.17), channel_id=1, source_target_pairs={{16,1},{1,16},{18,3},{3,18},{20,5},{5,20},{22,7},{7,22},{24,9},{9,... | collective-permute-start | bytes 393224 | tf_op jit(solution)/shard_map/ppermute | solution.py:309
  43.0 2.2 %all-gather.3 = bf16[4,2,128,256]{3,2,1,0:T(8,128)(2,1)S(1)} all-gather(bf16[2,2,128,256]{3,2,1,0:T(8,128)(2,1)S(1)} %get-tuple-element.16), channel_id=5, replica_groups={{0,1},{2,3},{4,5},{6,7},{8,9},{10,11},{12,13},{14,15},{16,17},{18,19},{..., dimensions={0}, use_global_device_ids=true | all-gather | bytes 786432 | tf_op jit(solution)/shard_map/all_gather | solution.py:248
  45.3 3.1 %collective-permute-start.6 = (bf16[2,128,256]{2,1,0:T(8,128)(2,1)S(1)}, bf16[2,128,256]{2,1,0:T(8,128)(2,1)S(1)}, u32[]{:S(2)}, u32[]{:S(2)}) collective-permute-start(bf16[2,128,256]{2,1,0:T(8,128)(2,1)S(1)} %shard_map.148), channel_id=1, source_target_pairs={{2,1},{1,2},{4,3},{3,4},{6,5},{5,6},{8,7},{7,8},{10,9},{9,10},{12,... | collective-permute-start | bytes 393224 | tf_op jit(solution)/shard_map/ppermute | solution.py:308
  48.3 8.9 %collective-permute-start.4 = (bf16[128,256]{1,0:T(8,128)(2,1)S(1)}, bf16[128,256]{1,0:T(8,128)(2,1)S(1)}, u32[]{:S(2)}, u32[]{:S(2)}) collective-permute-start(bf16[128,256]{1,0:T(8,128)(2,1)S(1)} %get-tuple-element.18), channel_id=1, source_target_pairs={{18,1},{1,18},{20,3},{3,20},{22,5},{5,22},{24,7},{7,24},{26,9},{9,... | collective-permute-start | bytes 196616 | tf_op jit(solution)/shard_map/ppermute | solution.py:310
  57.2 0.0 copy-start.2
  57.2 2.1 %collective-permute-start.5 = (bf16[128,256]{1,0:T(8,128)(2,1)S(1)}, bf16[128,256]{1,0:T(8,128)(2,1)S(1)}, u32[]{:S(2)}, u32[]{:S(2)}) collective-permute-start(bf16[128,256]{1,0:T(8,128)(2,1)S(1)} %get-tuple-element.19), channel_id=1, source_target_pairs={{0,1010},{1,31},{2,1012},{3,17},{4,1014},{5,19},{6,1016},{7,21},{8... | collective-permute-start | bytes 196616 | tf_op jit(solution)/shard_map/ppermute | solution.py:311
  59.3 0.0 collective-permute-done.3.remote
  59.3 2.0 %all-gather.4 = bf16[4,128,256]{2,1,0:T(8,128)(2,1)S(1)} all-gather(bf16[2,128,256]{2,1,0:T(8,128)(2,1)S(1)} %collective-permute-done.3.remote), channel_id=6, replica_groups={{0,1},{2,3},{4,5},{6,7},{8,9},{10,11},{12,13},{14,15},{16,17},{18,19},{..., dimensions={0}, use_global_device_ids=true | all-gather | bytes 393216 | tf_op jit(solution)/shard_map/all_gather | solution.py:248
  61.3 0.0 collective-permute-done.4.corner_near
  61.3 5.2 %collective-permute-done.5.corner_far = bf16[128,256]{1,0:T(8,128)(2,1)S(1)} collective-permute-done((bf16[128,256]{1,0:T(8,128)(2,1)S(1)}, bf16[128,256]{1,0:T(8,128)(2,1)S(1)}, u32[]{:S(2)}, u32[]{:S(2)}) %collective-permute-start.5) | collective-permute-done | bytes 65568 | tf_op jit(solution)/shard_map/ppermute | solution.py:311
  66.5 0.0 collective-permute-done.6.side
  66.5 0.0 copy-done.2
  66.6 0.7 copy-done.11
  67.2 1.0 %shard_map.149 = bf16[2,1,128,256]{3,2,1,0:T(8,128)(2,1)} custom-call(bf16[2,1,128,256]{3,2,1,0:T(8,128)(2,1)S(1)} %copy-done, f32[2,128,256]{2,1,0:T(8,128)S(1)} %get-tuple-element.15.owned, bf16[2,2,2,128,256]{4,3,2,1,0:T(8,128)(2,1)S(1)} %bitcast.12, bf16[2,128,256]{2,1,0:T(8,128)(2,1)S(1)} %collective-permute-done.3.remote, ...), custom_call_target="tpu_custom_call" | custom-call | tf_op jit(solution)/shard_map/pallas_call | solution.py:191
  (10 shorter events, 0.1 us)
Async XLA Ops:
  0.0 18.6 %collective-permute-start = (bf16[2,1,128,256]{3,2,1,0:T(8,128)(2,1)}, bf16[2,1,128,256]{3,2,1,0:T(8,128)(2,1)S(1)}, u32[]{:S(2)}, u32[]{:S(2)}) collective-permute-start(bf16[2,1,128,256]{3,2,1,0:T(8,128)(2,1)} %state.1), channel_id=1, source_target_pairs={{2,1},{1,2},{4,3},{3,4},{6,5},{5,6},{8,7},{7,8},{10,9},{9,10},{12,... | collective-permute-start | bytes 393224 | tf_op jit(solution)/shard_map/ppermute | solution.py:256
  7.3 30.8 %collective-permute-start.1 = (bf16[2,128,256]{2,1,0:T(8,128)(2,1)S(1)}, bf16[2,128,256]{2,1,0:T(8,128)(2,1)S(1)}, u32[]{:S(2)}, u32[]{:S(2)}) collective-permute-start(bf16[2,128,256]{2,1,0:T(8,128)(2,1)S(1)} %dynamic-slice_bitcast_fusion.1), channel_id=1, source_target_pairs={{16,1},{1,16},{18,3},{3,18},{20,5},{5,20},{22,7},{7,22},{24,9},{9,... | collective-permute-start | bytes 393224 | tf_op jit(solution)/shard_map/ppermute | solution.py:258
  20.6 11.5 %copy-start.13 = (s32[2,1]{0,1:T(1,128)S(1)}, s32[2,1]{0,1:T(1,128)}, u32[]{:S(2)}) copy-start(s32[2,1]{0,1:T(1,128)} %param.19) | copy-start | bytes 28
  20.6 11.7 %copy-start.5 = (s32[2,1,2,1024]{3,2,1,0:T(2,128)S(1)}, s32[2,1,2,1024]{3,2,1,0:T(2,128)}, u32[]{:S(2)}) copy-start(s32[2,1,2,1024]{3,2,1,0:T(2,128)} %index_t.1) | copy-start | bytes 49156
  20.6 11.7 %copy-start.6 = (s32[2,1,2,512]{3,2,1,0:T(2,128)S(1)}, s32[2,1,2,512]{3,2,1,0:T(2,128)}, u32[]{:S(2)}) copy-start(s32[2,1,2,512]{3,2,1,0:T(2,128)} %index_e.1) | copy-start | bytes 24580
  20.6 11.7 %copy-start.7 = (f32[2,1,1024]{2,1,0:T(1,128)S(1)}, f32[2,1,1024]{2,1,0:T(1,128)}, u32[]{:S(2)}) copy-start(f32[2,1,1024]{2,1,0:T(1,128)} %cosine.1) | copy-start | bytes 24580
  20.6 11.7 %copy-start.9 = (f32[2,1,512]{2,1,0:T(1,128)S(1)}, f32[2,1,512]{2,1,0:T(1,128)}, u32[]{:S(2)}) copy-start(f32[2,1,512]{2,1,0:T(1,128)} %dist.1) | copy-start | bytes 12292
  20.6 14.8 %copy-start.3 = (bf16[256,256]{1,0:T(8,128)(2,1)S(1)}, bf16[256,256]{1,0:T(8,128)(2,1)}, u32[]{:S(2)}) copy-start(bf16[256,256]{1,0:T(8,128)(2,1)} %w_centre.1) | copy-start | bytes 393220
  20.6 11.6 %copy-start.14 = (s32[2,1]{0,1:T(1,128)S(1)}, s32[2,1]{0,1:T(1,128)}, u32[]{:S(2)}) copy-start(s32[2,1]{0,1:T(1,128)} %param.22) | copy-start | bytes 28
  20.6 17.5 %collective-permute-start.2 = (bf16[2,128,256]{2,1,0:T(8,128)(2,1)S(1)}, bf16[2,128,256]{2,1,0:T(8,128)(2,1)S(1)}, u32[]{:S(2)}, u32[]{:S(2)}) collective-permute-start(bf16[2,128,256]{2,1,0:T(8,128)(2,1)S(1)} %dynamic-slice_bitcast_fusion), channel_id=1, source_target_pairs={{16,1},{1,16},{18,3},{3,18},{20,5},{5,20},{22,7},{7,22},{24,9},{9,... | collective-permute-start | bytes 393224 | tf_op jit(solution)/shard_map/ppermute | solution.py:260
  32.2 0.7 copy-start.10
  32.9 2.5 %copy-start = (bf16[2,1,128,256]{3,2,1,0:T(8,128)(2,1)S(1)}, bf16[2,1,128,256]{3,2,1,0:T(8,128)(2,1)}, u32[]{:S(2)}) copy-start(bf16[2,1,128,256]{3,2,1,0:T(8,128)(2,1)} %state.1) | copy-start | bytes 393220
  32.9 2.5 %copy-start.1 = (bf16[256,256]{1,0:T(8,128)(2,1)S(1)}, bf16[256,256]{1,0:T(8,128)(2,1)}, u32[]{:S(2)}) copy-start(bf16[256,256]{1,0:T(8,128)(2,1)} %w_neigh.3) | copy-start | bytes 393220
  33.5 1.9 %copy-start.8 = (f32[4,256]{1,0:T(4,128)S(1)}, f32[4,256]{1,0:T(4,128)}, u32[]{:S(2)}) copy-start(f32[4,256]{1,0:T(4,128)} %bias.1) | copy-start | bytes 12292
  35.4 0.7 copy-start.12
  36.1 2.1 %copy-start.4 = (bf16[256,256]{1,0:T(8,128)(2,1)S(1)}, bf16[256,256]{1,0:T(8,128)(2,1)}, u32[]{:S(2)}) copy-start(bf16[256,256]{1,0:T(8,128)(2,1)} %w_mix.1) | copy-start | bytes 393220
  40.4 19.0 %collective-permute-start.3 = (bf16[2,128,256]{2,1,0:T(8,128)(2,1)S(1)}, bf16[2,128,256]{2,1,0:T(8,128)(2,1)S(1)}, u32[]{:S(2)}, u32[]{:S(2)}) collective-permute-start(bf16[2,128,256]{2,1,0:T(8,128)(2,1)S(1)} %get-tuple-element.17), channel_id=1, source_target_pairs={{16,1},{1,16},{18,3},{3,18},{20,5},{5,20},{22,7},{7,22},{24,9},{9,... | collective-permute-start | bytes 393224 | tf_op jit(solution)/shard_map/ppermute | solution.py:309
  45.3 21.3 %collective-permute-start.6 = (bf16[2,128,256]{2,1,0:T(8,128)(2,1)S(1)}, bf16[2,128,256]{2,1,0:T(8,128)(2,1)S(1)}, u32[]{:S(2)}, u32[]{:S(2)}) collective-permute-start(bf16[2,128,256]{2,1,0:T(8,128)(2,1)S(1)} %shard_map.148), channel_id=1, source_target_pairs={{2,1},{1,2},{4,3},{3,4},{6,5},{5,6},{8,7},{7,8},{10,9},{9,10},{12,... | collective-permute-start | bytes 393224 | tf_op jit(solution)/shard_map/ppermute | solution.py:308
  48.3 13.0 %collective-permute-start.4 = (bf16[128,256]{1,0:T(8,128)(2,1)S(1)}, bf16[128,256]{1,0:T(8,128)(2,1)S(1)}, u32[]{:S(2)}, u32[]{:S(2)}) collective-permute-start(bf16[128,256]{1,0:T(8,128)(2,1)S(1)} %get-tuple-element.18), channel_id=1, source_target_pairs={{18,1},{1,18},{20,3},{3,20},{22,5},{5,22},{24,7},{7,24},{26,9},{9,... | collective-permute-start | bytes 196616 | tf_op jit(solution)/shard_map/ppermute | solution.py:310
  57.2 9.3 %copy-start.2 = (bf16[256,256]{1,0:T(8,128)(2,1)S(1)}, bf16[256,256]{1,0:T(8,128)(2,1)}, u32[]{:S(2)}) copy-start(bf16[256,256]{1,0:T(8,128)(2,1)} %w_out.1) | copy-start | bytes 393220
  57.2 9.3 %collective-permute-start.5 = (bf16[128,256]{1,0:T(8,128)(2,1)S(1)}, bf16[128,256]{1,0:T(8,128)(2,1)S(1)}, u32[]{:S(2)}, u32[]{:S(2)}) collective-permute-start(bf16[128,256]{1,0:T(8,128)(2,1)S(1)} %get-tuple-element.19), channel_id=1, source_target_pairs={{0,1010},{1,31},{2,1012},{3,17},{4,1014},{5,19},{6,1016},{7,21},{8... | collective-permute-start | bytes 196616 | tf_op jit(solution)/shard_map/ppermute | solution.py:311
  66.5 0.7 copy-start.11

commit v2 on v1

v2 whole, which is shorter than its diff:
```python
import functools

import jax
import jax.numpy as jnp
from jax import lax
from jax.experimental import pallas as pl
from jax.experimental.pallas import tpu as pltpu
from jax.sharding import PartitionSpec as P


F32 = jnp.float32
BF16 = jnp.bfloat16
NT = (((1,), (1,)), ((), ()))
TN = (((0,), (0,)), ((), ()))
VMEM_LIMIT = 32 * 1024 * 1024
VMEM_ALL = 63 * 1024 * 1024
LINES = 32


def core_bit():
    return lax.rem(lax.axis_index("gy"), 2)


def dot(left, right, dims=(((1,), (0,)), ((), ()))):
    return lax.dot_general(left, right, dims, preferred_element_type=F32)


def onehot(index, first, count):
    rows = lax.broadcasted_iota(jnp.int32, (count, index.shape[1]), 0) + first
    return jnp.where(rows == index, 1.0, 0.0).astype(BF16)


def fields(block, edges, trips, atoms, core):
    lines = block.astype(F32)
    width = lines.shape[1]
    at = 0

    def take(length):
        nonlocal at
        count = length // width
        parts = [lines[at + i : at + i + 1] for i in range(count)]
        at += count
        return jnp.concatenate(parts, axis=1)

    half = float(edges // 2)
    recv = (take(trips) + half).astype(jnp.int32)
    partner = (take(trips) + half).astype(jnp.int32)
    weight = take(trips)
    centre = take(edges).astype(jnp.int32)
    cell = take(edges)
    cell = jnp.where(core == 1, 8.0 - cell, cell)
    code = (cell * float(atoms) + take(edges)).astype(jnp.int32)
    reach = take(edges)
    reach = reach + take(edges)
    kind = lines[at : at + 1, 0:atoms]
    return recv, partner, weight, centre, code, reach, kind


def pack_kernel(
    count_e_hbm,
    count_t_hbm,
    state_hbm,
    index_e_hbm,
    dist_hbm,
    index_t_hbm,
    cosine_hbm,
    species_hbm,
    out,
    lines,
    count_e,
    count_t,
    index_e,
    dist,
    index_t,
    cosine,
    species,
    sems,
):
    edges = dist.shape[2]
    trips = cosine.shape[2]
    atoms = species.shape[2]
    width = lines.shape[1]
    half = edges // 2
    copies = [
        (count_e_hbm, count_e),
        (count_t_hbm, count_t),
        (index_e_hbm, index_e),
        (dist_hbm, dist),
        (index_t_hbm, index_t),
        (cosine_hbm, cosine),
        (species_hbm, species),
    ]
    copies += [(state_hbm.at[row, 0], out.at[row, pl.ds(0, atoms)]) for row in range(2)]
    copies = [
        pltpu.make_async_copy(source, target, sems.at[i])
        for i, (source, target) in enumerate(copies)
    ]
    for copy in copies:
        copy.start()
    lanes_e = lax.broadcasted_iota(jnp.int32, (1, edges), 1)
    lanes_t = lax.broadcasted_iota(jnp.int32, (1, trips), 1)
    for copy in copies:
        copy.wait()
    for row in range(2):
        at = 0

        def put(values):
            nonlocal at
            for first in range(0, values.shape[1], width):
                lines[at : at + 1, :] = values[:, first : first + width]
                at += 1

        lines[...] = jnp.zeros(lines.shape, F32)
        put((index_t[row, 0, 0:1, :] - half).astype(F32))
        put((index_t[row, 0, 1:2, :] - half).astype(F32))
        put(jnp.where(lanes_t < count_t[row], cosine[row], 0.0))
        put(index_e[row, 0, 0:1, :].astype(F32))
        code = index_e[row, 0, 1:2, :].astype(F32)
        cell = jnp.floor(code * (1.0 / atoms))
        put(cell)
        put(code - cell * float(atoms))
        reach = jnp.where(lanes_e < count_e[row], dist[row], 1.0)
        upper = reach.astype(BF16).astype(F32)
        put(upper)
        put(reach - upper)
        lines[at : at + 1, 0:atoms] = species[row].astype(F32)
        out[row, atoms : atoms + LINES] = lines[...].astype(BF16)


def link_matrix(recv, partner, weight, edges):
    into = onehot(recv, 0, edges)
    rows = lax.broadcasted_iota(jnp.int32, (edges, recv.shape[1]), 0)
    out_of = jnp.where(rows == partner, weight, 0.0).astype(BF16)
    return dot(out_of, into, NT).astype(BF16)


def scalar_columns(rows128, bias, radial):
    kinds = bias.shape[0]
    rows128[...] = jnp.zeros(rows128.shape, F32)
    rows128[0:kinds, :] = bias[...]
    rows128[kinds : kinds + 1, :] = radial[...]
    return jnp.transpose(rows128[...])


def centre_split(centre_t, states, kind, columns, kinds):
    proj = dot(centre_t, states, NT)
    for s in range(kinds):
        proj = proj + jnp.where(kind == float(s), columns[:, s : s + 1], 0.0)
    upper = proj.astype(BF16)
    return upper, (proj - upper.astype(F32)).astype(BF16)


def mine_kernel(
    trips,
    pack,
    edge_col,
    pair_edge,
    w_neigh,
    w_centre,
    w_out,
    gain,
    bias,
    radial,
    links,
    pre,
    near,
    w_out_kept,
    gain_kept,
    rows128,
):
    w_out_kept[...] = w_out[...]
    gain_kept[...] = gain[...]
    core = core_bit()
    far = 1 - core
    edges = links.shape[1]
    atoms = edge_col.shape[2]
    kinds = bias.shape[0]
    columns = scalar_columns(rows128, bias, radial)
    neigh_t = jnp.transpose(w_neigh[...])
    centre_t = jnp.transpose(w_centre[...])

    def row_states(row):
        return [
            edge_col[row, 0],
            pack[core, row, 0:atoms],
            pack[far, row, 0:atoms],
            pair_edge[far, row, 0],
        ]

    mine = row_states(core)
    rows = [
        dot(neigh_t, jnp.concatenate(states, axis=0), NT).astype(BF16)
        for states in (mine, row_states(far))
    ]
    near[...] = rows[0]
    for tile in range(2):
        holder = core if tile == 0 else far
        recv, partner, weight, centre, code, reach, kind = fields(
            pack[holder, core, atoms:], edges, trips, atoms, core
        )
        links[tile] = link_matrix(recv, partner, weight, edges)
        upper, lower = centre_split(centre_t, mine[1 + tile], kind, columns, kinds)
        span = slice(tile * atoms, (tile + 3) * atoms)
        values = jnp.concatenate([rows[0][:, span], rows[1][:, span], upper, lower], axis=1)
        pick_centre = onehot(centre, 0, atoms)
        picks = jnp.concatenate(
            [onehot(code, 3 * atoms, 6 * atoms), pick_centre, pick_centre], axis=0
        )
        pre[tile] = dot(values, picks) + columns[:, kinds : kinds + 1] * reach


def remote_kernel(trips, remote, w_centre, bias, radial, links, pre, rows128):
    core = core_bit()
    far = 1 - core
    edges = links.shape[1]
    atoms = remote.shape[2] - LINES
    kinds = bias.shape[0]
    columns = scalar_columns(rows128, bias, radial)
    centre_t = jnp.transpose(w_centre[...])
    for tile in range(2):
        holder = core if tile == 0 else far
        recv, partner, weight, centre, _, reach, kind = fields(
            remote[holder, far, atoms:], edges, trips, atoms, core
        )
        links[tile] = link_matrix(recv, partner, weight, edges)
        states = remote[holder, far, 0:atoms]
        values = jnp.concatenate(centre_split(centre_t, states, kind, columns, kinds), axis=1)
        pick_centre = onehot(centre, 0, atoms)
        picks = jnp.concatenate([pick_centre, pick_centre], axis=0)
        pre[tile] = dot(values, picks) + columns[:, kinds : kinds + 1] * reach


def edge_kernel(
    trips,
    pack,
    remote,
    remote_edge,
    links_mine,
    pre_mine,
    near_mine,
    links_remote,
    pre_remote,
    w_neigh,
    w_mix,
    post,
    side,
    owned,
):
    core = core_bit()
    far = 1 - core
    edges = links_mine.shape[1]
    atoms = owned.shape[1]
    neigh_t = jnp.transpose(w_neigh[...])
    mix_t = jnp.transpose(w_mix[...])

    def remote_row(row):
        states = [
            remote_edge[core, row, 0],
            remote[core, row, 0:atoms],
            remote[far, row, 0:atoms],
            remote_edge[far, row, 0],
        ]
        return dot(neigh_t, jnp.concatenate(states, axis=0), NT).astype(BF16)

    near_next = remote_row(far)
    near_last = remote_row(core)
    near_own = near_mine[...]
    spreads = []
    for source, row, links, pre, nears, kept in (
        (pack, core, links_mine, pre_mine, (near_next,), 3),
        (remote, far, links_remote, pre_remote, (near_last, near_next, near_own), 6),
    ):
        for tile in range(2):
            holder = core if tile == 0 else far
            _, _, _, _, code, reach, _ = fields(
                source[holder, row, atoms:], edges, trips, atoms, core
            )
            pick = onehot(code, 0, 9 * atoms)
            span = slice(tile * atoms, (tile + 3) * atoms)
            values = jnp.concatenate([near[:, span] for near in nears], axis=1)
            total = pre[tile] + dot(values, pick[0 : values.shape[1]])
            envelope = (1.0 - reach * reach) ** 2
            feat = (0.5 * total * (1.0 + jnp.tanh(0.5 * total)) * envelope).astype(BF16)
            mixed = dot(mix_t, feat).astype(BF16)
            message = (feat.astype(F32) * dot(mixed, links[tile])).astype(BF16)
            spreads.append(dot(pick[kept * atoms :], message, NT))

    def cell(row, slot):
        total = None
        for tile in range(2):
            if 0 <= slot - tile < 3:
                parts = [spreads[tile][(3 * row + slot - tile) * atoms :][:atoms]]
                if row == 0:
                    parts.append(spreads[2 + tile][(slot - tile) * atoms :][:atoms])
                for part in parts:
                    total = part if total is None else total + part
        return total

    for row, at in ((0, core), (1, far)):
        side[at] = cell(row, 0).astype(BF16)
        owned[at] = cell(row, 1)
        post[0, at] = cell(row, 2).astype(BF16)
        post[1, at] = cell(row, 3).astype(BF16)


def side_kernel(side, posts, out):
    far = 1 - core_bit()
    out[...] = (side[...].astype(F32) + posts[far, 1].astype(F32)).astype(BF16)


def final_kernel(pack, owned, posts, side, gain, w_out, out):
    core = core_bit()
    far = 1 - core
    atoms = owned.shape[1]
    for row in range(2):
        total = owned[row] + posts[far, 0, row].astype(F32) + side[row].astype(F32)
        scale = lax.rsqrt(jnp.mean(total * total, axis=-1, keepdims=True) + 1e-05)
        normed = (total * scale * gain[...]).astype(BF16)
        out[row, 0] = (
            pack[core, row, 0:atoms].astype(F32) + dot(normed, w_out[...])
        ).astype(BF16)


VMEM = pl.BlockSpec(memory_space=pltpu.VMEM)


HBM = pl.BlockSpec(memory_space=pltpu.HBM)


def call(kernel, outs, *operands, scratch=(), specs=None, limit=VMEM_LIMIT):
    return pl.pallas_call(
        kernel,
        out_shape=outs,
        in_specs=specs or [VMEM] * len(operands),
        out_specs=jax.tree.map(lambda _: VMEM, outs),
        scratch_shapes=list(scratch),
        compiler_params=pltpu.CompilerParams(vmem_limit_bytes=limit),
    )(*operands)


def pairings():
    count_x, count_y = lax.axis_size("gx"), lax.axis_size("gy")
    along_y, along_x = [], []
    for y in range(0, count_y, 2):
        first, second = (y + 2) % count_y, y + 1
        along_y += [(first, second), (second, first)]
    for x in range(count_x):
        for y in range(0, count_y, 2):
            first, second = (x + 1) % count_x * count_y + y, x * count_y + y + 1
            along_x += [(first, second), (second, first)]
    chips = [[y, y + 1] for y in range(0, count_y, 2)]
    return along_y, along_x, chips


def body(
    state,
    species,
    species_bias,
    edge_index,
    edge_count,
    edge_dist,
    trip_index,
    trip_count,
    trip_cos,
    radial_weight,
    norm_gain,
    w_centre,
    w_neigh,
    w_mix,
    w_out,
):
    size_x, _, atoms, chans = state.shape
    edges = edge_index.shape[3]
    trips = trip_index.shape[3]
    along_y, along_x, chips = pairings()
    both = ("gx", "gy")

    def gathered(value):
        return lax.all_gather(value, "gy", axis_index_groups=chips)

    def shaped(*shape, dtype=BF16):
        return jax.ShapeDtypeStruct(shape, dtype)

    edge_col = lax.ppermute(state, "gy", along_y)
    packed = call(
        pack_kernel,
        shaped(size_x, atoms + LINES, chans),
        edge_count.reshape(size_x),
        trip_count.reshape(size_x),
        state,
        edge_index,
        edge_dist,
        trip_index,
        trip_cos,
        species,
        specs=[HBM] * 8,
        limit=VMEM_ALL,
        scratch=[
            pltpu.VMEM((LINES, chans), F32),
            pltpu.SMEM((size_x,), jnp.int32),
            pltpu.SMEM((size_x,), jnp.int32),
            *(
                pltpu.VMEM(each.shape, each.dtype)
                for each in (edge_index, edge_dist, trip_index, trip_cos, species)
            ),
            pltpu.SemaphoreType.DMA((9,)),
        ],
    )
    pack = gathered(packed)
    remote = lax.ppermute(pack, both, along_x)
    pair_edge = gathered(edge_col)
    remote_edge = lax.ppermute(pair_edge, both, along_x)
    radial = radial_weight.reshape(1, chans)
    links = shaped(2, edges, edges)
    pre = shaped(2, chans, edges, dtype=F32)
    links_mine, pre_mine, near_mine, w_out, gain = call(
        functools.partial(mine_kernel, trips),
        (
            links,
            pre,
            shaped(chans, 4 * atoms),
            shaped(*w_out.shape),
            shaped(1, chans, dtype=F32),
        ),
        pack,
        edge_col,
        pair_edge,
        w_neigh,
        w_centre,
        w_out,
        norm_gain.reshape(1, chans),
        species_bias,
        radial,
        scratch=[pltpu.VMEM((128, chans), F32)],
    )
    links_remote, pre_remote = call(
        functools.partial(remote_kernel, trips),
        (links, pre),
        remote,
        w_centre,
        species_bias,
        radial,
        scratch=[pltpu.VMEM((128, chans), F32)],
    )
    tile = (atoms, chans)
    post, side, owned = call(
        functools.partial(edge_kernel, trips),
        (shaped(2, 2, *tile), shaped(2, *tile), shaped(2, *tile, dtype=F32)),
        pack,
        remote,
        remote_edge,
        links_mine,
        pre_mine,
        near_mine,
        links_remote,
        pre_remote,
        w_neigh,
        w_mix,
    )
    posts = gathered(post)
    side_in = lax.ppermute(call(side_kernel, shaped(2, *tile), side, posts), "gy", along_y)
    return call(
        final_kernel,
        shaped(*state.shape),
        pack,
        owned,
        posts,
        side_in,
        gain,
        w_out,
    )


def solution(mesh):
    placed = (
        P("gx", "gy", None, None),
        P("gx", "gy", None),
        P(),
        P("gx", "gy", None, None),
        P("gx", "gy"),
        P("gx", "gy", None),
        P("gx", "gy", None, None),
        P("gx", "gy"),
        P("gx", "gy", None),
        P(),
        P(),
        P(),
        P(),
        P(),
        P(),
    )
    return jax.shard_map(
        body, mesh=mesh, in_specs=placed, out_specs=P("gx", "gy", None, None), check_vma=False
    )
```

time: 68.6 us -> 58.4 us (0.85)
  the two profiles are of different devices: /device:TPU:32 before, /device:TPU:1 now
where the time goes in v2:
time: 58.4 us; the launch traced here: 58.1 us
  blocking collectives  30.5 us (52%)
  starting transfers between devices  10.6 us (18%)
  Pallas kernels  10.6 us (18%)
  waiting for transfers between devices  5.54 us (9%)
  local copies, waits for them, and re-layouts  0.65 us (1%)
    all_gather x3, blocking collectives, gathered(): return lax.all_gather(value, 'gy', axis_index_groups=chips)  30.5 us
    pallas_call x6, Pallas kernels, call(): pl.pallas_call(kernel, out_shape=outs, in_specs=specs or [VMEM] * len(ope...  10.6 us
    ppermute x1, starting transfers between devices, body(): edge_col = lax.ppermute(state, 'gy', along_y)  4.58 us
    ppermute x1, waiting for transfers between devices, body(): lax.ppermute(call(side_kernel, shaped(2, *tile), side, posts), 'gy', alon...  4.36 us
    ppermute x1, starting transfers between devices, body(): remote = lax.ppermute(pack, both, along_x)  2.04 us
    ppermute x1, starting transfers between devices, body(): remote_edge = lax.ppermute(pair_edge, both, along_x)  2.04 us
    ppermute x1, starting transfers between devices, body(): lax.ppermute(call(side_kernel, shaped(2, *tile), side, posts), 'gy', alon...  1.92 us
    ppermute x1, waiting for transfers between devices, body(): remote_edge = lax.ppermute(pair_edge, both, along_x)  1.18 us
  transfers between devices with their start and end apart: 4, of which 2 were waited for; matrix products, arithmetic and copies ran while one was open for 0% of the time, Pallas kernels for 10%

profile of v2, /device:TPU:1, one launch (start us, length us, event | category | flops | bytes accessed | tf_op | source)
XLA Modules:
  0.0 58.1 jit_solution(13304313006840618482)
XLA Ops:
  0.0 4.6 %collective-permute-start.1 = (bf16[2,1,128,256]{3,2,1,0:T(8,128)(2,1)}, bf16[2,1,128,256]{3,2,1,0:T(8,128)(2,1)S(1)}, u32[]{:S(2)}, u32[]{:S(2)}) collective-permute-start(bf16[2,1,128,256]{3,2,1,0:T(8,128)(2,1)} %state_hbm.1), channel_id=1, source_target_pairs={{2,1},{1,2},{4,3},{3,4},{6,5},{5,6},{8,7},{7,8},{10,9},{9,10},{12,... | collective-permute-start | bytes 393224 | tf_op jit(solution)/shard_map/ppermute | solution.py:384
  4.6 1.7 %shard_map.145 = bf16[2,160,256]{2,1,0:T(8,128)(2,1)} custom-call(s32[2]{0:T(128)} %bitcast.18, s32[2]{0:T(128)} %bitcast.19, bf16[2,1,128,256]{3,2,1,0:T(8,128)(2,1)} %state_hbm.1, s32[2,1,2,512]{3,2,1,0:T(2,128)} %index_e_hbm.1, f32[2,1,512]{2,1,0:T(1,128)} %dist_hbm.1, s32[2,1,2,1024]{3,2,1,0:T(2,128)} %index_t_hbm.1, f32[2,1,1024]{2,1,0:T(1,128)} %cosine_hbm.1, ...), custom_call_target="tpu_custom_call" | custom-call | tf_op jit(solution)/shard_map/pallas_call | solution.py:331
  6.3 0.0 copy-start.6
  6.4 13.4 %all-gather = bf16[4,160,256]{2,1,0:T(8,128)(2,1)S(1)} all-gather(bf16[2,160,256]{2,1,0:T(8,128)(2,1)} %shard_map.145), channel_id=2, replica_groups={{0,1},{2,3},{4,5},{6,7},{8,9},{10,11},{12,13},{14,15},{16,17},{18,19},{..., dimensions={0}, use_global_device_ids=true | all-gather | bytes 491520 | tf_op jit(solution)/shard_map/all_gather | solution.py:379
  19.7 0.0 copy-start
  19.7 0.0 copy-start.1
  19.7 0.0 copy-start.2
  19.7 2.0 %collective-permute-start = (bf16[2,2,160,256]{3,2,1,0:T(8,128)(2,1)S(1)}, bf16[2,2,160,256]{3,2,1,0:T(8,128)(2,1)S(1)}, u32[]{:S(2)}, u32[]{:S(2)}) collective-permute-start(bf16[2,2,160,256]{3,2,1,0:T(8,128)(2,1)S(1)} %bitcast.7), channel_id=1, source_target_pairs={{16,1},{1,16},{18,3},{3,18},{20,5},{5,20},{22,7},{7,22},{24,9},{9,... | collective-permute-start | bytes 983048 | tf_op jit(solution)/shard_map/ppermute | solution.py:410
  21.8 0.0 collective-permute-done.1.edge_col
  21.8 11.4 %all-gather.1 = bf16[4,1,128,256]{3,2,1,0:T(8,128)(2,1)S(1)} all-gather(bf16[2,1,128,256]{3,2,1,0:T(8,128)(2,1)S(1)} %collective-permute-done.1.edge_col), channel_id=3, replica_groups={{0,1},{2,3},{4,5},{6,7},{8,9},{10,11},{12,13},{14,15},{16,17},{18,19},{..., dimensions={0}, use_global_device_ids=true | all-gather | bytes 393216 | tf_op jit(solution)/shard_map/all_gather | solution.py:379
  33.2 0.0 copy-start.4
  33.2 2.0 %collective-permute-start.2 = (bf16[2,2,1,128,256]{4,3,2,1,0:T(8,128)(2,1)S(1)}, bf16[2,2,1,128,256]{4,3,2,1,0:T(8,128)(2,1)S(1)}, u32[]{:S(2)}, u32[]{:S(2)}) collective-permute-start(bf16[2,2,1,128,256]{4,3,2,1,0:T(8,128)(2,1)S(1)} %bitcast.13), channel_id=1, source_target_pairs={{16,1},{1,16},{18,3},{3,18},{20,5},{5,20},{22,7},{7,22},{24,9},{9,... | collective-permute-start | bytes 786440 | tf_op jit(solution)/shard_map/ppermute | solution.py:412
  35.2 0.0 copy-start.5
  35.2 0.0 copy-done.6
  35.2 0.0 copy-done
  35.3 0.0 copy-done.1
  35.3 0.0 copy-done.2
  35.3 0.0 copy-done.4
  35.3 0.6 %copy-done.5 = f32[256]{0:T(256)S(1)} copy-done((f32[256]{0:T(256)S(1)}, f32[256]{0:T(256)}, u32[]{:S(2)}) %copy-start.5) | copy-done | bytes 1048
  35.9 2.1 %shard_map.146 = (bf16[2,512,512]{2,1,0:T(8,128)(2,1)S(1)}, f32[2,256,512]{2,1,0:T(8,128)S(1)}, bf16[256,512]{1,0:T(8,128)(2,1)S(1)}, bf16[256,256]{1,0:T(8,128)(2,1)S(1)}, f32[1,256]{1,0:T(1,128)S(1)}) custom-call(bf16[2,2,160,256]{3,2,1,0:T(8,128)(2,1)S(1)} %bitcast.8, bf16[2,1,128,256]{3,2,1,0:T(8,128)(2,1)S(1)} %collective-permute-done.1.edge_col, ...), custom_call_target="tpu_custom_call" | custom-call | tf_op jit(solution)/shard_map/pallas_call | solution.py:331
  38.0 0.0 copy-start.3
  38.0 0.0 collective-permute-done.remote
  38.0 1.8 %shard_map.147 = (bf16[2,512,512]{2,1,0:T(8,128)(2,1)S(1)}, f32[2,256,512]{2,1,0:T(8,128)S(1)}) custom-call(bf16[2,2,160,256]{3,2,1,0:T(8,128)(2,1)S(1)} %collective-permute-done.remote, bf16[256,256]{1,0:T(8,128)(2,1)S(1)} %copy-done, f32[4,256]{1,0:T(4,128)S(1)} %copy-done.4, f32[1,256]{1,0:T(1,128)S(1)} %bitcast.16), custom_call_target="tpu_custom_call" | custom-call | tf_op jit(solution)/shard_map/pallas_call | solution.py:331
  39.8 1.2 %collective-permute-done.2.remote_edge = bf16[2,2,1,128,256]{4,3,2,1,0:T(8,128)(2,1)S(1)} collective-permute-done((bf16[2,2,1,128,256]{4,3,2,1,0:T(8,128)(2,1)S(1)}, bf16[2,2,1,128,256]{4,3,2,1,0:T(8,128)(2,1)S(1)}, u32[]{:S(2)}, u32[]{:S(2)}) %collective-permute-start.2) | collective-permute-done | bytes 262176 | tf_op jit(solution)/shard_map/ppermute | solution.py:412
  41.0 0.0 copy-done.3
  41.0 4.0 %shard_map.148 = (bf16[2,2,128,256]{3,2,1,0:T(8,128)(2,1)S(1)}, bf16[2,128,256]{2,1,0:T(8,128)(2,1)S(1)}, f32[2,128,256]{2,1,0:T(8,128)S(1)}) custom-call(bf16[2,2,160,256]{3,2,1,0:T(8,128)(2,1)S(1)} %bitcast.9, bf16[2,2,160,256]{3,2,1,0:T(8,128)(2,1)S(1)} %collective-permute-done.remote, ...), custom_call_target="tpu_custom_call" | custom-call | tf_op jit(solution)/shard_map/pallas_call | solution.py:331
  45.0 5.8 %all-gather.2 = bf16[4,2,128,256]{3,2,1,0:T(8,128)(2,1)S(1)} all-gather(bf16[2,2,128,256]{3,2,1,0:T(8,128)(2,1)S(1)} %get-tuple-element.21), channel_id=4, replica_groups={{0,1},{2,3},{4,5},{6,7},{8,9},{10,11},{12,13},{14,15},{16,17},{18,19},{..., dimensions={0}, use_global_device_ids=true | all-gather | bytes 786432 | tf_op jit(solution)/shard_map/all_gather | solution.py:379
  50.8 1.9 %collective-permute-start.3 = (bf16[2,128,256]{2,1,0:T(8,128)(2,1)S(1)}, bf16[2,128,256]{2,1,0:T(8,128)(2,1)S(1)}, u32[]{:S(2)}, u32[]{:S(2)}) collective-permute-start(bf16[2,128,256]{2,1,0:T(8,128)(2,1)S(1)} %shard_map.149), channel_id=1, source_target_pairs={{2,1},{1,2},{4,3},{3,4},{6,5},{5,6},{8,7},{7,8},{10,9},{9,10},{12,... | collective-permute-start | bytes 393224 | tf_op jit(solution)/shard_map/ppermute | solution.py:461
  52.8 4.4 %collective-permute-done.3.side = bf16[2,128,256]{2,1,0:T(8,128)(2,1)S(1)} collective-permute-done((bf16[2,128,256]{2,1,0:T(8,128)(2,1)S(1)}, bf16[2,128,256]{2,1,0:T(8,128)(2,1)S(1)}, u32[]{:S(2)}, u32[]{:S(2)}) %collective-permute-start.3) | collective-permute-done | bytes 131104 | tf_op jit(solution)/shard_map/ppermute | solution.py:461
  57.1 0.9 %shard_map.150 = bf16[2,1,128,256]{3,2,1,0:T(8,128)(2,1)} custom-call(bf16[2,2,160,256]{3,2,1,0:T(8,128)(2,1)S(1)} %bitcast.10, f32[2,128,256]{2,1,0:T(8,128)S(1)} %get-tuple-element.20.owned, bf16[2,2,2,128,256]{4,3,2,1,0:T(8,128)(2,1)S(1)} %bitcast.12, bf16[2,128,256]{2,1,0:T(8,128)(2,1)S(1)} %collective-permute-done.3.side, ...), custom_call_target="tpu_custom_call" | custom-call | tf_op jit(solution)/shard_map/pallas_call | solution.py:331
  (1 shorter events, 0.0 us)
Async XLA Ops:
  0.0 21.8 %collective-permute-start.1 = (bf16[2,1,128,256]{3,2,1,0:T(8,128)(2,1)}, bf16[2,1,128,256]{3,2,1,0:T(8,128)(2,1)S(1)}, u32[]{:S(2)}, u32[]{:S(2)}) collective-permute-start(bf16[2,1,128,256]{3,2,1,0:T(8,128)(2,1)} %state_hbm.1), channel_id=1, source_target_pairs={{2,1},{1,2},{4,3},{3,4},{6,5},{5,6},{8,7},{7,8},{10,9},{9,10},{12,... | collective-permute-start | bytes 393224 | tf_op jit(solution)/shard_map/ppermute | solution.py:384
  6.3 28.9 %copy-start.6 = (f32[256]{0:T(256)S(1)}, f32[256]{0:T(256)}, u32[]{:S(2)}) copy-start(f32[256]{0:T(256)} %param.25) | copy-start | bytes 3076
  19.7 15.5 %copy-start = (bf16[256,256]{1,0:T(8,128)(2,1)S(1)}, bf16[256,256]{1,0:T(8,128)(2,1)}, u32[]{:S(2)}) copy-start(bf16[256,256]{1,0:T(8,128)(2,1)} %w_centre.3) | copy-start | bytes 393220
  19.7 15.5 %copy-start.1 = (bf16[256,256]{1,0:T(8,128)(2,1)S(1)}, bf16[256,256]{1,0:T(8,128)(2,1)}, u32[]{:S(2)}) copy-start(bf16[256,256]{1,0:T(8,128)(2,1)} %w_neigh.3) | copy-start | bytes 393220
  19.7 15.5 %copy-start.2 = (bf16[256,256]{1,0:T(8,128)(2,1)S(1)}, bf16[256,256]{1,0:T(8,128)(2,1)}, u32[]{:S(2)}) copy-start(bf16[256,256]{1,0:T(8,128)(2,1)} %w_out.1) | copy-start | bytes 393220
  19.7 18.3 %collective-permute-start = (bf16[2,2,160,256]{3,2,1,0:T(8,128)(2,1)S(1)}, bf16[2,2,160,256]{3,2,1,0:T(8,128)(2,1)S(1)}, u32[]{:S(2)}, u32[]{:S(2)}) collective-permute-start(bf16[2,2,160,256]{3,2,1,0:T(8,128)(2,1)S(1)} %bitcast.7), channel_id=1, source_target_pairs={{16,1},{1,16},{18,3},{3,18},{20,5},{5,20},{22,7},{7,22},{24,9},{9,... | collective-permute-start | bytes 983048 | tf_op jit(solution)/shard_map/ppermute | solution.py:410
  33.2 2.1 %copy-start.4 = (f32[4,256]{1,0:T(4,128)S(1)}, f32[4,256]{1,0:T(4,128)}, u32[]{:S(2)}) copy-start(f32[4,256]{1,0:T(4,128)} %bias.3) | copy-start | bytes 12292
  33.2 7.8 %collective-permute-start.2 = (bf16[2,2,1,128,256]{4,3,2,1,0:T(8,128)(2,1)S(1)}, bf16[2,2,1,128,256]{4,3,2,1,0:T(8,128)(2,1)S(1)}, u32[]{:S(2)}, u32[]{:S(2)}) collective-permute-start(bf16[2,2,1,128,256]{4,3,2,1,0:T(8,128)(2,1)S(1)} %bitcast.13), channel_id=1, source_target_pairs={{16,1},{1,16},{18,3},{3,18},{20,5},{5,20},{22,7},{7,22},{24,9},{9,... | collective-permute-start | bytes 786440 | tf_op jit(solution)/shard_map/ppermute | solution.py:412
  35.2 0.7 %copy-start.5 = (f32[256]{0:T(256)S(1)}, f32[256]{0:T(256)}, u32[]{:S(2)}) copy-start(f32[256]{0:T(256)} %param.24) | copy-start | bytes 3076
  38.0 3.0 %copy-start.3 = (bf16[256,256]{1,0:T(8,128)(2,1)S(1)}, bf16[256,256]{1,0:T(8,128)(2,1)}, u32[]{:S(2)}) copy-start(bf16[256,256]{1,0:T(8,128)(2,1)} %w_mix.1) | copy-start | bytes 393220
  50.8 6.3 %collective-permute-start.3 = (bf16[2,128,256]{2,1,0:T(8,128)(2,1)S(1)}, bf16[2,128,256]{2,1,0:T(8,128)(2,1)S(1)}, u32[]{:S(2)}, u32[]{:S(2)}) collective-permute-start(bf16[2,128,256]{2,1,0:T(8,128)(2,1)S(1)} %shard_map.149), channel_id=1, source_target_pairs={{2,1},{1,2},{4,3},{3,4},{6,5},{5,6},{8,7},{7,8},{10,9},{9,10},{12,... | collective-permute-start | bytes 393224 | tf_op jit(solution)/shard_map/ppermute | solution.py:461

commit v3 on v2

--- a/solution.py
+++ b/solution.py
@@ -14,7 +14,7 @@
 TN = (((0,), (0,)), ((), ()))
 VMEM_LIMIT = 32 * 1024 * 1024
 VMEM_ALL = 63 * 1024 * 1024
-LINES = 32
+LINES = 48
 
 
 def core_bit():
@@ -28,6 +28,14 @@
 def onehot(index, first, count):
     rows = lax.broadcasted_iota(jnp.int32, (count, index.shape[1]), 0) + first
     return jnp.where(rows == index, 1.0, 0.0).astype(BF16)
+
+
+def blocked_onehot(low, high, blocks, size, values=1.0):
+    base = onehot(low, 0, size)
+    return jnp.concatenate(
+        [base * jnp.where(high == b, values, 0.0).astype(BF16) for b in blocks],
+        axis=0,
+    )
 
 
 def fields(block, edges, trips, atoms, core):
@@ -49,11 +57,12 @@
     centre = take(edges).astype(jnp.int32)
     cell = take(edges)
     cell = jnp.where(core == 1, 8.0 - cell, cell)
-    code = (cell * float(atoms) + take(edges)).astype(jnp.int32)
+    cell = cell.astype(jnp.int32)
+    slot = take(edges).astype(jnp.int32)
     reach = take(edges)
     reach = reach + take(edges)
     kind = lines[at : at + 1, 0:atoms]
-    return recv, partner, weight, centre, code, reach, kind
+    return recv, partner, weight, centre, cell, slot, reach, kind, lines[at + 1 :]
 
 
 def pack_kernel(
@@ -65,6 +74,8 @@
     index_t_hbm,
     cosine_hbm,
     species_hbm,
+    bias_hbm,
+    radial_hbm,
     out,
     lines,
     count_e,
@@ -74,6 +85,8 @@
     index_t,
     cosine,
     species,
+    bias,
+    radial,
     sems,
 ):
     edges = dist.shape[2]
@@ -89,6 +102,8 @@
         (index_t_hbm, index_t),
         (cosine_hbm, cosine),
         (species_hbm, species),
+        (bias_hbm, bias),
+        (radial_hbm, radial),
     ]
     copies += [(state_hbm.at[row, 0], out.at[row, pl.ds(0, atoms)]) for row in range(2)]
     copies = [
@@ -124,21 +139,33 @@
         put(upper)
         put(reach - upper)
         lines[at : at + 1, 0:atoms] = species[row].astype(F32)
+        at += 1
+        for values in (bias[...], radial[...]):
+            upper = values.astype(BF16).astype(F32)
+            for each in (upper, values - upper):
+                lines[at : at + values.shape[0], :] = each
+                at += values.shape[0]
         out[row, atoms : atoms + LINES] = lines[...].astype(BF16)
 
 
-def link_matrix(recv, partner, weight, edges):
-    into = onehot(recv, 0, edges)
-    rows = lax.broadcasted_iota(jnp.int32, (edges, recv.shape[1]), 0)
-    out_of = jnp.where(rows == partner, weight, 0.0).astype(BF16)
+def link_matrix(recv, partner, weight, edges, atoms):
+    blocks = range(edges // atoms)
+
+    def parts(index):
+        high = lax.div(index, atoms)
+        return index - high * atoms, high
+
+    into = blocked_onehot(*parts(recv), blocks, atoms)
+    out_of = blocked_onehot(*parts(partner), blocks, atoms, weight)
     return dot(out_of, into, NT).astype(BF16)
 
 
-def scalar_columns(rows128, bias, radial):
-    kinds = bias.shape[0]
+def scalar_columns(rows128, lines, kinds):
+    bias = lines[0:kinds] + lines[kinds : 2 * kinds]
+    radial = lines[2 * kinds : 2 * kinds + 1] + lines[2 * kinds + 1 : 2 * kinds + 2]
     rows128[...] = jnp.zeros(rows128.shape, F32)
-    rows128[0:kinds, :] = bias[...]
-    rows128[kinds : kinds + 1, :] = radial[...]
+    rows128[0:kinds, :] = bias
+    rows128[kinds : kinds + 1, :] = radial
     return jnp.transpose(rows128[...])
 
 
@@ -152,6 +179,7 @@
 
 def mine_kernel(
     trips,
+    kinds,
     pack,
     edge_col,
     pair_edge,
@@ -159,8 +187,6 @@
     w_centre,
     w_out,
     gain,
-    bias,
-    radial,
     links,
     pre,
     near,
@@ -174,8 +200,8 @@
     far = 1 - core
     edges = links.shape[1]
     atoms = edge_col.shape[2]
-    kinds = bias.shape[0]
-    columns = scalar_columns(rows128, bias, radial)
+    scalars = fields(pack[core, core, atoms:], edges, trips, atoms, core)[-1]
+    columns = scalar_columns(rows128, scalars, kinds)
     neigh_t = jnp.transpose(w_neigh[...])
     centre_t = jnp.transpose(w_centre[...])
 
@@ -195,39 +221,84 @@
     near[...] = rows[0]
     for tile in range(2):
         holder = core if tile == 0 else far
-        recv, partner, weight, centre, code, reach, kind = fields(
+        recv, partner, weight, centre, cell, slot, reach, kind, _ = fields(
             pack[holder, core, atoms:], edges, trips, atoms, core
         )
-        links[tile] = link_matrix(recv, partner, weight, edges)
+        links[tile] = link_matrix(recv, partner, weight, edges, atoms)
         upper, lower = centre_split(centre_t, mine[1 + tile], kind, columns, kinds)
         span = slice(tile * atoms, (tile + 3) * atoms)
         values = jnp.concatenate([rows[0][:, span], rows[1][:, span], upper, lower], axis=1)
         pick_centre = onehot(centre, 0, atoms)
         picks = jnp.concatenate(
-            [onehot(code, 3 * atoms, 6 * atoms), pick_centre, pick_centre], axis=0
+            [blocked_onehot(slot, cell, range(3, 9), atoms), pick_centre, pick_centre], axis=0
         )
         pre[tile] = dot(values, picks) + columns[:, kinds : kinds + 1] * reach
 
 
-def remote_kernel(trips, remote, w_centre, bias, radial, links, pre, rows128):
+def inner_slots(tile):
+    return [slot for slot in (1, 2) if 0 <= slot - tile < 3]
+
+
+def remote_kernel(
+    trips,
+    kinds,
+    pack,
+    remote,
+    pre_mine,
+    near_mine,
+    w_neigh,
+    w_centre,
+    links,
+    pre_mine_out,
+    pre,
+    rows128,
+):
     core = core_bit()
     far = 1 - core
     edges = links.shape[1]
     atoms = remote.shape[2] - LINES
-    kinds = bias.shape[0]
-    columns = scalar_columns(rows128, bias, radial)
+    scalars = fields(remote[core, far, atoms:], edges, trips, atoms, core)[-1]
+    columns = scalar_columns(rows128, scalars, kinds)
+    neigh_t = jnp.transpose(w_neigh[...])
     centre_t = jnp.transpose(w_centre[...])
+    near_last, near_next = [
+        dot(
+            neigh_t,
+            jnp.concatenate([remote[core, row, 0:atoms], remote[far, row, 0:atoms]], axis=0),
+            NT,
+        ).astype(BF16)
+        for row in (core, far)
+    ]
+    near_own = near_mine[...]
     for tile in range(2):
         holder = core if tile == 0 else far
-        recv, partner, weight, centre, _, reach, kind = fields(
+        recv, partner, weight, centre, cell, slot, reach, kind, _ = fields(
             remote[holder, far, atoms:], edges, trips, atoms, core
         )
-        links[tile] = link_matrix(recv, partner, weight, edges)
+        links[tile] = link_matrix(recv, partner, weight, edges, atoms)
         states = remote[holder, far, 0:atoms]
-        values = jnp.concatenate(centre_split(centre_t, states, kind, columns, kinds), axis=1)
+        inner = [at - tile for at in inner_slots(tile)]
+        span = slice(tile * atoms, (tile + 3) * atoms)
+        values = jnp.concatenate(
+            [
+                near_last,
+                near_next,
+                near_own[:, span],
+                *centre_split(centre_t, states, kind, columns, kinds),
+            ],
+            axis=1,
+        )
         pick_centre = onehot(centre, 0, atoms)
-        picks = jnp.concatenate([pick_centre, pick_centre], axis=0)
+        blocks = inner + [3 + at for at in inner] + [6, 7, 8]
+        picks = jnp.concatenate(
+            [blocked_onehot(slot, cell, blocks, atoms), pick_centre, pick_centre], axis=0
+        )
         pre[tile] = dot(values, picks) + columns[:, kinds : kinds + 1] * reach
+        _, _, _, _, cell, slot, _, _, _ = fields(
+            pack[holder, core, atoms:], edges, trips, atoms, core
+        )
+        picks = blocked_onehot(slot, cell, inner, atoms)
+        pre_mine_out[tile] = pre_mine[tile] + dot(near_next, picks)
 
 
 def edge_kernel(
@@ -237,7 +308,6 @@
     remote_edge,
     links_mine,
     pre_mine,
-    near_mine,
     links_remote,
     pre_remote,
     w_neigh,
@@ -250,40 +320,30 @@
     far = 1 - core
     edges = links_mine.shape[1]
     atoms = owned.shape[1]
-    neigh_t = jnp.transpose(w_neigh[...])
     mix_t = jnp.transpose(w_mix[...])
-
-    def remote_row(row):
-        states = [
-            remote_edge[core, row, 0],
-            remote[core, row, 0:atoms],
-            remote[far, row, 0:atoms],
-            remote_edge[far, row, 0],
-        ]
-        return dot(neigh_t, jnp.concatenate(states, axis=0), NT).astype(BF16)
-
-    near_next = remote_row(far)
-    near_last = remote_row(core)
-    near_own = near_mine[...]
+    corners = [remote_edge[core, core, 0], remote_edge[core, far, 0]]
+    corners += [remote_edge[far, core, 0], remote_edge[far, far, 0]]
+    near = dot(jnp.transpose(w_neigh[...]), jnp.concatenate(corners, axis=0), NT).astype(BF16)
     spreads = []
-    for source, row, links, pre, nears, kept in (
-        (pack, core, links_mine, pre_mine, (near_next,), 3),
-        (remote, far, links_remote, pre_remote, (near_last, near_next, near_own), 6),
+    for source, row, links, pre, outer, kept in (
+        (pack, core, links_mine, pre_mine, (0,), range(3, 9)),
+        (remote, far, links_remote, pre_remote, (0, 3), range(6, 9)),
     ):
         for tile in range(2):
             holder = core if tile == 0 else far
-            _, _, _, _, code, reach, _ = fields(
+            _, _, _, _, cells, slots, reach, _, _ = fields(
                 source[holder, row, atoms:], edges, trips, atoms, core
             )
-            pick = onehot(code, 0, 9 * atoms)
-            span = slice(tile * atoms, (tile + 3) * atoms)
-            values = jnp.concatenate([near[:, span] for near in nears], axis=1)
-            total = pre[tile] + dot(values, pick[0 : values.shape[1]])
+            blocks = [first + 2 * tile for first in outer] + list(kept)
+            pick = blocked_onehot(slots, cells, blocks, atoms)
+            values = near[:, (2 * tile + 2 - len(outer)) * atoms : (2 * tile + 2) * atoms]
+            depth = len(outer) * atoms
+            total = pre[tile] + dot(values, pick[0:depth])
             envelope = (1.0 - reach * reach) ** 2
             feat = (0.5 * total * (1.0 + jnp.tanh(0.5 * total)) * envelope).astype(BF16)
             mixed = dot(mix_t, feat).astype(BF16)
             message = (feat.astype(F32) * dot(mixed, links[tile])).astype(BF16)
-            spreads.append(dot(pick[kept * atoms :], message, NT))
+            spreads.append(dot(pick[depth:], message, NT))
 
     def cell(row, slot):
         total = None
@@ -313,7 +373,7 @@
     far = 1 - core
     atoms = owned.shape[1]
     for row in range(2):
-        total = owned[row] + posts[far, 0, row].astype(F32) + side[row].astype(F32)
+        total = owned[row] + posts[far, 0, row].astype(F32) + side[far, row].astype(F32)
         scale = lax.rsqrt(jnp.mean(total * total, axis=-1, keepdims=True) + 1e-05)
         normed = (total * scale * gain[...]).astype(BF16)
         out[row, 0] = (
@@ -372,6 +432,7 @@
     size_x, _, atoms, chans = state.shape
     edges = edge_index.shape[3]
     trips = trip_index.shape[3]
+    kinds = species_bias.shape[0]
     along_y, along_x, chips = pairings()
     both = ("gx", "gy")
 
@@ -382,6 +443,7 @@
         return jax.ShapeDtypeStruct(shape, dtype)
 
     edge_col = lax.ppermute(state, "gy", along_y)
+    radial = radial_weight.reshape(1, chans)
     packed = call(
         pack_kernel,
         shaped(size_x, atoms + LINES, chans),
@@ -393,7 +455,9 @@
         trip_index,
         trip_cos,
         species,
-        specs=[HBM] * 8,
+        species_bias,
+        radial,
+        specs=[HBM] * 10,
         limit=VMEM_ALL,
         scratch=[
             pltpu.VMEM((LINES, chans), F32),
@@ -401,20 +465,27 @@
             pltpu.SMEM((size_x,), jnp.int32),
             *(
                 pltpu.VMEM(each.shape, each.dtype)
-                for each in (edge_index, edge_dist, trip_index, trip_cos, species)
+                for each in (
+                    edge_index,
+                    edge_dist,
+                    trip_index,
+                    trip_cos,
+                    species,
+                    species_bias,
+                    radial,
+                )
             ),
-            pltpu.SemaphoreType.DMA((9,)),
+            pltpu.SemaphoreType.DMA((11,)),
         ],
     )
     pack = gathered(packed)
     remote = lax.ppermute(pack, both, along_x)
     pair_edge = gathered(edge_col)
     remote_edge = lax.ppermute(pair_edge, both, along_x)
-    radial = radial_weight.reshape(1, chans)
     links = shaped(2, edges, edges)
     pre = shaped(2, chans, edges, dtype=F32)
     links_mine, pre_mine, near_mine, w_out, gain = call(
-        functools.partial(mine_kernel, trips),
+        functools.partial(mine_kernel, trips, kinds),
         (
             links,
             pre,
@@ -429,17 +500,17 @@
         w_centre,
         w_out,
         norm_gain.reshape(1, chans),
-        species_bias,
-        radial,
         scratch=[pltpu.VMEM((128, chans), F32)],
     )
-    links_remote, pre_remote = call(
-        functools.partial(remote_kernel, trips),
-        (links, pre),
+    links_remote, pre_mine, pre_remote = call(
+        functools.partial(remote_kernel, trips, kinds),
+        (links, pre, pre),
+        pack,
         remote,
+        pre_mine,
+        near_mine,
+        w_neigh,
         w_centre,
-        species_bias,
-        radial,
         scratch=[pltpu.VMEM((128, chans), F32)],
     )
     tile = (atoms, chans)
@@ -451,14 +522,14 @@
         remote_edge,
         links_mine,
         pre_mine,
-        near_mine,
         links_remote,
         pre_remote,
         w_neigh,
         w_mix,
     )
     posts = gathered(post)
-    side_in = lax.ppermute(call(side_kernel, shaped(2, *tile), side, posts), "gy", along_y)
+    side_out = call(side_kernel, shaped(2, *tile), side, posts)
+    side_in = lax.all_gather(side_out, "gy", axis_index_groups=[list(pair) for pair in along_y[::2]])
     return call(
         final_kernel,
         shaped(*state.shape),

time: 58.4 us -> 56.5 us (0.967)
  blocking collectives: 30.5 us -> 35.9 us
  waiting for transfers between devices: 5.54 us -> 1.27 us
  starting transfers between devices: 10.6 us -> 8.66 us
  local copies, waits for them, and re-layouts: 0.65 us -> 0.02 us
    all_gather x0 -> x1, blocking collectives: none -> 5.36 us  [body(): lax.all_gather(side_out, 'gy', axis_index_groups=[list(pair) for pair in...]
    ppermute x1 -> x0, waiting for transfers between devices: 4.36 us -> none  [body(): lax.ppermute(call(side_kernel, shaped(2, *tile), side, posts), 'gy', alon...]
    ppermute x1 -> x0, starting transfers between devices: 1.92 us -> none  [body(): lax.ppermute(call(side_kernel, shaped(2, *tile), side, posts), 'gy', alon...]
    unnamed x14 -> x10, local copies, waits for them, and re-layouts: 0.65 us -> 0.02 us
  transfers between devices with their start and end apart: 4 -> 3, of which waited for: 2 -> 1; matrix products, arithmetic and copies ran while one was open for 0% -> 0% of each run, Pallas kernels for 10% -> 11%
where the time goes in v3:
time: 56.5 us; the launch traced here: 56.2 us
  blocking collectives  35.9 us (64%)
  Pallas kernels  10.2 us (18%)
  starting transfers between devices  8.66 us (15%)
  waiting for transfers between devices  1.27 us (2%)
    all_gather x3, blocking collectives, gathered(): return lax.all_gather(value, 'gy', axis_index_groups=chips)  30.6 us
    pallas_call x6, Pallas kernels, call(): pl.pallas_call(kernel, out_shape=outs, in_specs=specs or [VMEM] * len(ope...  10.2 us
    all_gather x1, blocking collectives, body(): lax.all_gather(side_out, 'gy', axis_index_groups=[list(pair) for pair in...  5.36 us
    ppermute x1, starting transfers between devices, body(): edge_col = lax.ppermute(state, 'gy', along_y)  4.58 us
    ppermute x1, starting transfers between devices, body(): remote = lax.ppermute(pack, both, along_x)  2.04 us
    ppermute x1, starting transfers between devices, body(): remote_edge = lax.ppermute(pair_edge, both, along_x)  2.04 us
    ppermute x1, waiting for transfers between devices, body(): remote_edge = lax.ppermute(pair_edge, both, along_x)  1.26 us
  transfers between devices with their start and end apart: 3, of which 1 were waited for; matrix products, arithmetic and copies ran while one was open for 0% of the time, Pallas kernels for 11%

profile of v3, /device:TPU:1, one launch (start us, length us, event | category | flops | bytes accessed | tf_op | source)
XLA Modules:
  0.0 56.2 jit_solution(7281674686734067807)
XLA Ops:
  0.0 4.6 %collective-permute-start.1 = (bf16[2,1,128,256]{3,2,1,0:T(8,128)(2,1)}, bf16[2,1,128,256]{3,2,1,0:T(8,128)(2,1)S(1)}, u32[]{:S(2)}, u32[]{:S(2)}) collective-permute-start(bf16[2,1,128,256]{3,2,1,0:T(8,128)(2,1)} %state_hbm.1), channel_id=1, source_target_pairs={{2,1},{1,2},{4,3},{3,4},{6,5},{5,6},{8,7},{7,8},{10,9},{9,10},{12,... | collective-permute-start | bytes 393224 | tf_op jit(solution)/shard_map/ppermute | solution.py:445
  4.6 1.8 %shard_map.145 = bf16[2,176,256]{2,1,0:T(8,128)(2,1)} custom-call(s32[2]{0:T(128)} %bitcast.20, s32[2]{0:T(128)} %bitcast.21, bf16[2,1,128,256]{3,2,1,0:T(8,128)(2,1)} %state_hbm.1, s32[2,1,2,512]{3,2,1,0:T(2,128)} %index_e_hbm.1, f32[2,1,512]{2,1,0:T(1,128)} %dist_hbm.1, s32[2,1,2,1024]{3,2,1,0:T(2,128)} %index_t_hbm.1, f32[2,1,1024]{2,1,0:T(1,128)} %cosine_hbm.1, ...), custom_call_target="tpu_custom_call" | custom-call | tf_op jit(solution)/shard_map/pallas_call | solution.py:391
  6.4 13.4 %all-gather = bf16[4,176,256]{2,1,0:T(8,128)(2,1)S(1)} all-gather(bf16[2,176,256]{2,1,0:T(8,128)(2,1)} %shard_map.145), channel_id=2, replica_groups={{0,1},{2,3},{4,5},{6,7},{8,9},{10,11},{12,13},{14,15},{16,17},{18,19},{..., dimensions={0}, use_global_device_ids=true | all-gather | bytes 540672 | tf_op jit(solution)/shard_map/all_gather | solution.py:440
  19.8 0.0 copy-start
  19.8 0.0 copy-start.1
  19.8 0.0 copy-start.3
  19.8 2.0 %collective-permute-start = (bf16[2,2,176,256]{3,2,1,0:T(8,128)(2,1)S(1)}, bf16[2,2,176,256]{3,2,1,0:T(8,128)(2,1)S(1)}, u32[]{:S(2)}, u32[]{:S(2)}) collective-permute-start(bf16[2,2,176,256]{3,2,1,0:T(8,128)(2,1)S(1)} %bitcast.8), channel_id=1, source_target_pairs={{16,1},{1,16},{18,3},{3,18},{20,5},{5,20},{22,7},{7,22},{24,9},{9,... | collective-permute-start | bytes 1081352 | tf_op jit(solution)/shard_map/ppermute | solution.py:482
  21.8 0.0 collective-permute-done.1.edge_col
  21.9 11.4 %all-gather.1 = bf16[4,1,128,256]{3,2,1,0:T(8,128)(2,1)S(1)} all-gather(bf16[2,1,128,256]{3,2,1,0:T(8,128)(2,1)S(1)} %collective-permute-done.1.edge_col), channel_id=3, replica_groups={{0,1},{2,3},{4,5},{6,7},{8,9},{10,11},{12,13},{14,15},{16,17},{18,19},{..., dimensions={0}, use_global_device_ids=true | all-gather | bytes 393216 | tf_op jit(solution)/shard_map/all_gather | solution.py:440
  33.2 0.0 copy-start.4
  33.2 2.0 %collective-permute-start.2 = (bf16[2,2,1,128,256]{4,3,2,1,0:T(8,128)(2,1)S(1)}, bf16[2,2,1,128,256]{4,3,2,1,0:T(8,128)(2,1)S(1)}, u32[]{:S(2)}, u32[]{:S(2)}) collective-permute-start(bf16[2,2,1,128,256]{4,3,2,1,0:T(8,128)(2,1)S(1)} %bitcast.15), channel_id=1, source_target_pairs={{16,1},{1,16},{18,3},{3,18},{20,5},{5,20},{22,7},{7,22},{24,9},{9,... | collective-permute-start | bytes 786440 | tf_op jit(solution)/shard_map/ppermute | solution.py:484
  35.3 0.0 copy-done
  35.3 0.0 copy-done.1
  35.3 0.0 copy-done.3
  35.3 0.0 copy-done.4
  35.3 2.1 %shard_map.146 = (bf16[2,512,512]{2,1,0:T(8,128)(2,1)S(1)}, f32[2,256,512]{2,1,0:T(8,128)S(1)}, bf16[256,512]{1,0:T(8,128)(2,1)S(1)}, bf16[256,256]{1,0:T(8,128)(2,1)S(1)}, f32[1,256]{1,0:T(1,128)S(1)}) custom-call(bf16[2,2,176,256]{3,2,1,0:T(8,128)(2,1)S(1)} %bitcast.9, bf16[2,1,128,256]{3,2,1,0:T(8,128)(2,1)S(1)} %collective-permute-done.1.edge_col, ...), custom_call_target="tpu_custom_call" | custom-call | tf_op jit(solution)/shard_map/pallas_call | solution.py:391
  37.4 0.0 collective-permute-done.remote
  37.5 0.0 copy-start.2
  37.5 2.3 %shard_map.147 = (bf16[2,512,512]{2,1,0:T(8,128)(2,1)S(1)}, f32[2,256,512]{2,1,0:T(8,128)S(1)}, f32[2,256,512]{2,1,0:T(8,128)S(1)}) custom-call(bf16[2,2,176,256]{3,2,1,0:T(8,128)(2,1)S(1)} %bitcast.10, bf16[2,2,176,256]{3,2,1,0:T(8,128)(2,1)S(1)} %collective-permute-done.remote, f32[2,256,512]{2,1,0:T(8,128)S(1)} %get-tuple-element.17.pre_mine, ...), custom_call_target="tpu_custom_call" | custom-call | tf_op jit(solution)/shard_map/pallas_call | solution.py:391
  39.8 1.3 %collective-permute-done.2.remote_edge = bf16[2,2,1,128,256]{4,3,2,1,0:T(8,128)(2,1)S(1)} collective-permute-done((bf16[2,2,1,128,256]{4,3,2,1,0:T(8,128)(2,1)S(1)}, bf16[2,2,1,128,256]{4,3,2,1,0:T(8,128)(2,1)S(1)}, u32[]{:S(2)}, u32[]{:S(2)}) %collective-permute-start.2) | collective-permute-done | bytes 262176 | tf_op jit(solution)/shard_map/ppermute | solution.py:484
  41.1 0.0 copy-done.2
  41.1 3.0 %shard_map.148 = (bf16[2,2,128,256]{3,2,1,0:T(8,128)(2,1)S(1)}, bf16[2,128,256]{2,1,0:T(8,128)(2,1)S(1)}, f32[2,128,256]{2,1,0:T(8,128)S(1)}) custom-call(bf16[2,2,176,256]{3,2,1,0:T(8,128)(2,1)S(1)} %bitcast.11, bf16[2,2,176,256]{3,2,1,0:T(8,128)(2,1)S(1)} %collective-permute-done.remote, ...), custom_call_target="tpu_custom_call" | custom-call | tf_op jit(solution)/shard_map/pallas_call | solution.py:391
  44.1 5.8 %all-gather.2 = bf16[4,2,128,256]{3,2,1,0:T(8,128)(2,1)S(1)} all-gather(bf16[2,2,128,256]{3,2,1,0:T(8,128)(2,1)S(1)} %get-tuple-element.23), channel_id=4, replica_groups={{0,1},{2,3},{4,5},{6,7},{8,9},{10,11},{12,13},{14,15},{16,17},{18,19},{..., dimensions={0}, use_global_device_ids=true | all-gather | bytes 786432 | tf_op jit(solution)/shard_map/all_gather | solution.py:440
  49.9 5.4 %all-gather.3 = bf16[4,128,256]{2,1,0:T(8,128)(2,1)S(1)} all-gather(bf16[2,128,256]{2,1,0:T(8,128)(2,1)S(1)} %shard_map.149), channel_id=5, replica_groups={{2,1},{4,3},{6,5},{8,7},{10,9},{12,11},{14,13},{0,15},{18,17},{20,19},{..., dimensions={0}, use_global_device_ids=true | all-gather | bytes 393216 | tf_op jit(solution)/shard_map/all_gather | solution.py:532
  55.3 0.9 %shard_map.150 = bf16[2,1,128,256]{3,2,1,0:T(8,128)(2,1)} custom-call(bf16[2,2,176,256]{3,2,1,0:T(8,128)(2,1)S(1)} %bitcast.12, f32[2,128,256]{2,1,0:T(8,128)S(1)} %get-tuple-element.22.owned, bf16[2,2,2,128,256]{4,3,2,1,0:T(8,128)(2,1)S(1)} %bitcast.14, bf16[2,2,128,256]{3,2,1,0:T(8,128)(2,1)S(1)} %bitcast.17, f32[1,256]{1,0:T(1,128)S(1)} %get-tuple-element.25.gain, ...), custom_call_target="tpu_custom_call" | custom-call | tf_op jit(solution)/shard_map/pallas_call | solution.py:391
  (1 shorter events, 0.0 us)
Async XLA Ops:
  0.0 21.8 %collective-permute-start.1 = (bf16[2,1,128,256]{3,2,1,0:T(8,128)(2,1)}, bf16[2,1,128,256]{3,2,1,0:T(8,128)(2,1)S(1)}, u32[]{:S(2)}, u32[]{:S(2)}) collective-permute-start(bf16[2,1,128,256]{3,2,1,0:T(8,128)(2,1)} %state_hbm.1), channel_id=1, source_target_pairs={{2,1},{1,2},{4,3},{3,4},{6,5},{5,6},{8,7},{7,8},{10,9},{9,10},{12,... | collective-permute-start | bytes 393224 | tf_op jit(solution)/shard_map/ppermute | solution.py:445
  19.8 15.5 %copy-start = (bf16[256,256]{1,0:T(8,128)(2,1)S(1)}, bf16[256,256]{1,0:T(8,128)(2,1)}, u32[]{:S(2)}) copy-start(bf16[256,256]{1,0:T(8,128)(2,1)} %w_neigh.5) | copy-start | bytes 393220
  19.8 15.5 %copy-start.1 = (bf16[256,256]{1,0:T(8,128)(2,1)S(1)}, bf16[256,256]{1,0:T(8,128)(2,1)}, u32[]{:S(2)}) copy-start(bf16[256,256]{1,0:T(8,128)(2,1)} %w_centre.3) | copy-start | bytes 393220
  19.8 15.5 %copy-start.3 = (bf16[256,256]{1,0:T(8,128)(2,1)S(1)}, bf16[256,256]{1,0:T(8,128)(2,1)}, u32[]{:S(2)}) copy-start(bf16[256,256]{1,0:T(8,128)(2,1)} %w_out.1) | copy-start | bytes 393220
  19.8 17.6 %collective-permute-start = (bf16[2,2,176,256]{3,2,1,0:T(8,128)(2,1)S(1)}, bf16[2,2,176,256]{3,2,1,0:T(8,128)(2,1)S(1)}, u32[]{:S(2)}, u32[]{:S(2)}) collective-permute-start(bf16[2,2,176,256]{3,2,1,0:T(8,128)(2,1)S(1)} %bitcast.8), channel_id=1, source_target_pairs={{16,1},{1,16},{18,3},{3,18},{20,5},{5,20},{22,7},{7,22},{24,9},{9,... | collective-permute-start | bytes 1081352 | tf_op jit(solution)/shard_map/ppermute | solution.py:482
  33.2 2.1 %copy-start.4 = (f32[256]{0:T(256)S(1)}, f32[256]{0:T(256)}, u32[]{:S(2)}) copy-start(f32[256]{0:T(256)} %param.25) | copy-start | bytes 3076
  33.2 7.8 %collective-permute-start.2 = (bf16[2,2,1,128,256]{4,3,2,1,0:T(8,128)(2,1)S(1)}, bf16[2,2,1,128,256]{4,3,2,1,0:T(8,128)(2,1)S(1)}, u32[]{:S(2)}, u32[]{:S(2)}) collective-permute-start(bf16[2,2,1,128,256]{4,3,2,1,0:T(8,128)(2,1)S(1)} %bitcast.15), channel_id=1, source_target_pairs={{16,1},{1,16},{18,3},{3,18},{20,5},{5,20},{22,7},{7,22},{24,9},{9,... | collective-permute-start | bytes 786440 | tf_op jit(solution)/shard_map/ppermute | solution.py:484
  37.5 3.6 %copy-start.2 = (bf16[256,256]{1,0:T(8,128)(2,1)S(1)}, bf16[256,256]{1,0:T(8,128)(2,1)}, u32[]{:S(2)}) copy-start(bf16[256,256]{1,0:T(8,128)(2,1)} %w_mix.1) | copy-start | bytes 393220

commit v4 on v3

--- a/solution.py
+++ b/solution.py
@@ -114,7 +114,8 @@
         copy.start()
     lanes_e = lax.broadcasted_iota(jnp.int32, (1, edges), 1)
     lanes_t = lax.broadcasted_iota(jnp.int32, (1, trips), 1)
-    for copy in copies:
+    lines[...] = jnp.zeros(lines.shape, F32)
+    for copy in copies[:-2]:
         copy.wait()
     for row in range(2):
         at = 0
@@ -125,7 +126,6 @@
                 lines[at : at + 1, :] = values[:, first : first + width]
                 at += 1
 
-        lines[...] = jnp.zeros(lines.shape, F32)
         put((index_t[row, 0, 0:1, :] - half).astype(F32))
         put((index_t[row, 0, 1:2, :] - half).astype(F32))
         put(jnp.where(lanes_t < count_t[row], cosine[row], 0.0))
@@ -146,6 +146,8 @@
                 lines[at : at + values.shape[0], :] = each
                 at += values.shape[0]
         out[row, atoms : atoms + LINES] = lines[...].astype(BF16)
+    for copy in copies[-2:]:
+        copy.wait()
 
 
 def link_matrix(recv, partner, weight, edges, atoms):
@@ -324,26 +326,48 @@
     corners = [remote_edge[core, core, 0], remote_edge[core, far, 0]]
     corners += [remote_edge[far, core, 0], remote_edge[far, far, 0]]
     near = dot(jnp.transpose(w_neigh[...]), jnp.concatenate(corners, axis=0), NT).astype(BF16)
-    spreads = []
+    jobs = []
     for source, row, links, pre, outer, kept in (
         (pack, core, links_mine, pre_mine, (0,), range(3, 9)),
         (remote, far, links_remote, pre_remote, (0, 3), range(6, 9)),
     ):
         for tile in range(2):
-            holder = core if tile == 0 else far
-            _, _, _, _, cells, slots, reach, _, _ = fields(
-                source[holder, row, atoms:], edges, trips, atoms, core
-            )
-            blocks = [first + 2 * tile for first in outer] + list(kept)
-            pick = blocked_onehot(slots, cells, blocks, atoms)
-            values = near[:, (2 * tile + 2 - len(outer)) * atoms : (2 * tile + 2) * atoms]
-            depth = len(outer) * atoms
-            total = pre[tile] + dot(values, pick[0:depth])
-            envelope = (1.0 - reach * reach) ** 2
-            feat = (0.5 * total * (1.0 + jnp.tanh(0.5 * total)) * envelope).astype(BF16)
-            mixed = dot(mix_t, feat).astype(BF16)
-            message = (feat.astype(F32) * dot(mixed, links[tile])).astype(BF16)
-            spreads.append(dot(pick[depth:], message, NT))
+            jobs.append((source, row, links, pre, outer, kept, tile))
+    state = [{} for _ in jobs]
+
+    def gather_step(job, held):
+        source, row, _, pre, outer, kept, tile = job
+        holder = core if tile == 0 else far
+        _, _, _, _, cells, slots, reach, _, _ = fields(
+            source[holder, row, atoms:], edges, trips, atoms, core
+        )
+        blocks = [first + 2 * tile for first in outer] + list(kept)
+        pick = blocked_onehot(slots, cells, blocks, atoms)
+        values = near[:, (2 * tile + 2 - len(outer)) * atoms : (2 * tile + 2) * atoms]
+        depth = len(outer) * atoms
+        held["total"] = pre[tile] + dot(values, pick[0:depth])
+        held["pick"] = pick[depth:]
+        held["envelope"] = (1.0 - reach * reach) ** 2
+
+    def feature_step(job, held):
+        total = held["total"]
+        feat = (0.5 * total * (1.0 + jnp.tanh(0.5 * total)) * held["envelope"]).astype(BF16)
+        held["feat"] = feat
+        held["mixed"] = dot(mix_t, feat).astype(BF16)
+
+    def message_step(job, held):
+        message = held["feat"].astype(F32) * dot(held["mixed"], job[2][job[6]])
+        held["message"] = message.astype(BF16)
+
+    def spread_step(job, held):
+        held["spread"] = dot(held["pick"], held["message"], NT)
+
+    steps = (gather_step, feature_step, message_step, spread_step)
+    for turn in range(len(jobs) + len(steps) - 1):
+        for i, step in reversed(list(enumerate(steps))):
+            if 0 <= turn - i < len(jobs):
+                step(jobs[turn - i], state[turn - i])
+    spreads = [held["spread"] for held in state]
 
     def cell(row, slot):
         total = None

time: 56.5 us -> 55.8 us (0.988)
  Pallas kernels: 10.2 us -> 9.56 us
    pallas_call x6, Pallas kernels: 10.2 us -> 9.56 us  [call(): pl.pallas_call(kernel, out_shape=outs, in_specs=specs or [VMEM] * len(ope...]
where the time goes in v4:
time: 55.8 us; the launch traced here: 55.6 us
  blocking collectives  35.9 us (64%)
  Pallas kernels  9.56 us (17%)
  starting transfers between devices  8.66 us (16%)
  waiting for transfers between devices  1.27 us (2%)
    all_gather x3, blocking collectives, gathered(): return lax.all_gather(value, 'gy', axis_index_groups=chips)  30.6 us
    pallas_call x6, Pallas kernels, call(): pl.pallas_call(kernel, out_shape=outs, in_specs=specs or [VMEM] * len(ope...  9.56 us
    all_gather x1, blocking collectives, body(): lax.all_gather(side_out, 'gy', axis_index_groups=[list(pair) for pair in...  5.36 us
    ppermute x1, starting transfers between devices, body(): edge_col = lax.ppermute(state, 'gy', along_y)  4.58 us
    ppermute x1, starting transfers between devices, body(): remote = lax.ppermute(pack, both, along_x)  2.04 us
    ppermute x1, starting transfers between devices, body(): remote_edge = lax.ppermute(pair_edge, both, along_x)  2.04 us
    ppermute x1, waiting for transfers between devices, body(): remote_edge = lax.ppermute(pair_edge, both, along_x)  1.26 us
  transfers between devices with their start and end apart: 3, of which 1 were waited for; matrix products, arithmetic and copies ran while one was open for 0% of the time, Pallas kernels for 11%

profile of v4, /device:TPU:1, one launch (start us, length us, event | category | flops | bytes accessed | tf_op | source)
XLA Modules:
  0.0 55.6 jit_solution(17263255354891408590)
XLA Ops:
  0.0 4.6 %collective-permute-start.1 = (bf16[2,1,128,256]{3,2,1,0:T(8,128)(2,1)}, bf16[2,1,128,256]{3,2,1,0:T(8,128)(2,1)S(1)}, u32[]{:S(2)}, u32[]{:S(2)}) collective-permute-start(bf16[2,1,128,256]{3,2,1,0:T(8,128)(2,1)} %state_hbm.1), channel_id=1, source_target_pairs={{2,1},{1,2},{4,3},{3,4},{6,5},{5,6},{8,7},{7,8},{10,9},{9,10},{12,... | collective-permute-start | bytes 393224 | tf_op jit(solution)/shard_map/ppermute | solution.py:469
  4.6 1.8 %shard_map.145 = bf16[2,176,256]{2,1,0:T(8,128)(2,1)} custom-call(s32[2]{0:T(128)} %bitcast.20, s32[2]{0:T(128)} %bitcast.21, bf16[2,1,128,256]{3,2,1,0:T(8,128)(2,1)} %state_hbm.1, s32[2,1,2,512]{3,2,1,0:T(2,128)} %index_e_hbm.1, f32[2,1,512]{2,1,0:T(1,128)} %dist_hbm.1, s32[2,1,2,1024]{3,2,1,0:T(2,128)} %index_t_hbm.1, f32[2,1,1024]{2,1,0:T(1,128)} %cosine_hbm.1, ...), custom_call_target="tpu_custom_call" | custom-call | tf_op jit(solution)/shard_map/pallas_call | solution.py:415
  6.4 13.4 %all-gather = bf16[4,176,256]{2,1,0:T(8,128)(2,1)S(1)} all-gather(bf16[2,176,256]{2,1,0:T(8,128)(2,1)} %shard_map.145), channel_id=2, replica_groups={{0,1},{2,3},{4,5},{6,7},{8,9},{10,11},{12,13},{14,15},{16,17},{18,19},{..., dimensions={0}, use_global_device_ids=true | all-gather | bytes 540672 | tf_op jit(solution)/shard_map/all_gather | solution.py:464
  19.7 0.0 copy-start
  19.7 0.0 copy-start.1
  19.7 0.0 copy-start.3
  19.7 2.0 %collective-permute-start = (bf16[2,2,176,256]{3,2,1,0:T(8,128)(2,1)S(1)}, bf16[2,2,176,256]{3,2,1,0:T(8,128)(2,1)S(1)}, u32[]{:S(2)}, u32[]{:S(2)}) collective-permute-start(bf16[2,2,176,256]{3,2,1,0:T(8,128)(2,1)S(1)} %bitcast.8), channel_id=1, source_target_pairs={{16,1},{1,16},{18,3},{3,18},{20,5},{5,20},{22,7},{7,22},{24,9},{9,... | collective-permute-start | bytes 1081352 | tf_op jit(solution)/shard_map/ppermute | solution.py:506
  21.8 0.0 collective-permute-done.1.edge_col
  21.8 11.4 %all-gather.1 = bf16[4,1,128,256]{3,2,1,0:T(8,128)(2,1)S(1)} all-gather(bf16[2,1,128,256]{3,2,1,0:T(8,128)(2,1)S(1)} %collective-permute-done.1.edge_col), channel_id=3, replica_groups={{0,1},{2,3},{4,5},{6,7},{8,9},{10,11},{12,13},{14,15},{16,17},{18,19},{..., dimensions={0}, use_global_device_ids=true | all-gather | bytes 393216 | tf_op jit(solution)/shard_map/all_gather | solution.py:464
  33.2 0.0 copy-start.4
  33.2 2.0 %collective-permute-start.2 = (bf16[2,2,1,128,256]{4,3,2,1,0:T(8,128)(2,1)S(1)}, bf16[2,2,1,128,256]{4,3,2,1,0:T(8,128)(2,1)S(1)}, u32[]{:S(2)}, u32[]{:S(2)}) collective-permute-start(bf16[2,2,1,128,256]{4,3,2,1,0:T(8,128)(2,1)S(1)} %bitcast.15), channel_id=1, source_target_pairs={{16,1},{1,16},{18,3},{3,18},{20,5},{5,20},{22,7},{7,22},{24,9},{9,... | collective-permute-start | bytes 786440 | tf_op jit(solution)/shard_map/ppermute | solution.py:508
  35.2 0.0 copy-done
  35.3 0.0 copy-done.1
  35.3 0.0 copy-done.3
  35.3 0.0 copy-done.4
  35.3 2.1 %shard_map.146 = (bf16[2,512,512]{2,1,0:T(8,128)(2,1)S(1)}, f32[2,256,512]{2,1,0:T(8,128)S(1)}, bf16[256,512]{1,0:T(8,128)(2,1)S(1)}, bf16[256,256]{1,0:T(8,128)(2,1)S(1)}, f32[1,256]{1,0:T(1,128)S(1)}) custom-call(bf16[2,2,176,256]{3,2,1,0:T(8,128)(2,1)S(1)} %bitcast.9, bf16[2,1,128,256]{3,2,1,0:T(8,128)(2,1)S(1)} %collective-permute-done.1.edge_col, ...), custom_call_target="tpu_custom_call" | custom-call | tf_op jit(solution)/shard_map/pallas_call | solution.py:415
  37.4 0.0 collective-permute-done.remote
  37.4 0.0 copy-start.2
  37.4 2.3 %shard_map.147 = (bf16[2,512,512]{2,1,0:T(8,128)(2,1)S(1)}, f32[2,256,512]{2,1,0:T(8,128)S(1)}, f32[2,256,512]{2,1,0:T(8,128)S(1)}) custom-call(bf16[2,2,176,256]{3,2,1,0:T(8,128)(2,1)S(1)} %bitcast.10, bf16[2,2,176,256]{3,2,1,0:T(8,128)(2,1)S(1)} %collective-permute-done.remote, f32[2,256,512]{2,1,0:T(8,128)S(1)} %get-tuple-element.17.pre_mine, ...), custom_call_target="tpu_custom_call" | custom-call | tf_op jit(solution)/shard_map/pallas_call | solution.py:415
  39.8 1.3 %collective-permute-done.2.remote_edge = bf16[2,2,1,128,256]{4,3,2,1,0:T(8,128)(2,1)S(1)} collective-permute-done((bf16[2,2,1,128,256]{4,3,2,1,0:T(8,128)(2,1)S(1)}, bf16[2,2,1,128,256]{4,3,2,1,0:T(8,128)(2,1)S(1)}, u32[]{:S(2)}, u32[]{:S(2)}) %collective-permute-start.2) | collective-permute-done | bytes 262176 | tf_op jit(solution)/shard_map/ppermute | solution.py:508
  41.0 0.0 copy-done.2
  41.0 2.4 %shard_map.148 = (bf16[2,2,128,256]{3,2,1,0:T(8,128)(2,1)S(1)}, bf16[2,128,256]{2,1,0:T(8,128)(2,1)S(1)}, f32[2,128,256]{2,1,0:T(8,128)S(1)}) custom-call(bf16[2,2,176,256]{3,2,1,0:T(8,128)(2,1)S(1)} %bitcast.11, bf16[2,2,176,256]{3,2,1,0:T(8,128)(2,1)S(1)} %collective-permute-done.remote, ...), custom_call_target="tpu_custom_call" | custom-call | tf_op jit(solution)/shard_map/pallas_call | solution.py:415
  43.4 5.8 %all-gather.2 = bf16[4,2,128,256]{3,2,1,0:T(8,128)(2,1)S(1)} all-gather(bf16[2,2,128,256]{3,2,1,0:T(8,128)(2,1)S(1)} %get-tuple-element.23), channel_id=4, replica_groups={{0,1},{2,3},{4,5},{6,7},{8,9},{10,11},{12,13},{14,15},{16,17},{18,19},{..., dimensions={0}, use_global_device_ids=true | all-gather | bytes 786432 | tf_op jit(solution)/shard_map/all_gather | solution.py:464
  49.3 5.4 %all-gather.3 = bf16[4,128,256]{2,1,0:T(8,128)(2,1)S(1)} all-gather(bf16[2,128,256]{2,1,0:T(8,128)(2,1)S(1)} %shard_map.149), channel_id=5, replica_groups={{2,1},{4,3},{6,5},{8,7},{10,9},{12,11},{14,13},{0,15},{18,17},{20,19},{..., dimensions={0}, use_global_device_ids=true | all-gather | bytes 393216 | tf_op jit(solution)/shard_map/all_gather | solution.py:556
  54.6 0.9 %shard_map.150 = bf16[2,1,128,256]{3,2,1,0:T(8,128)(2,1)} custom-call(bf16[2,2,176,256]{3,2,1,0:T(8,128)(2,1)S(1)} %bitcast.12, f32[2,128,256]{2,1,0:T(8,128)S(1)} %get-tuple-element.22.owned, bf16[2,2,2,128,256]{4,3,2,1,0:T(8,128)(2,1)S(1)} %bitcast.14, bf16[2,2,128,256]{3,2,1,0:T(8,128)(2,1)S(1)} %bitcast.17, f32[1,256]{1,0:T(1,128)S(1)} %get-tuple-element.25.gain, ...), custom_call_target="tpu_custom_call" | custom-call | tf_op jit(solution)/shard_map/pallas_call | solution.py:415
  (1 shorter events, 0.0 us)
Async XLA Ops:
  0.0 21.8 %collective-permute-start.1 = (bf16[2,1,128,256]{3,2,1,0:T(8,128)(2,1)}, bf16[2,1,128,256]{3,2,1,0:T(8,128)(2,1)S(1)}, u32[]{:S(2)}, u32[]{:S(2)}) collective-permute-start(bf16[2,1,128,256]{3,2,1,0:T(8,128)(2,1)} %state_hbm.1), channel_id=1, source_target_pairs={{2,1},{1,2},{4,3},{3,4},{6,5},{5,6},{8,7},{7,8},{10,9},{9,10},{12,... | collective-permute-start | bytes 393224 | tf_op jit(solution)/shard_map/ppermute | solution.py:469
  19.7 15.5 %copy-start = (bf16[256,256]{1,0:T(8,128)(2,1)S(1)}, bf16[256,256]{1,0:T(8,128)(2,1)}, u32[]{:S(2)}) copy-start(bf16[256,256]{1,0:T(8,128)(2,1)} %w_neigh.5) | copy-start | bytes 393220
  19.7 15.5 %copy-start.1 = (bf16[256,256]{1,0:T(8,128)(2,1)S(1)}, bf16[256,256]{1,0:T(8,128)(2,1)}, u32[]{:S(2)}) copy-start(bf16[256,256]{1,0:T(8,128)(2,1)} %w_centre.3) | copy-start | bytes 393220
  19.7 15.5 %copy-start.3 = (bf16[256,256]{1,0:T(8,128)(2,1)S(1)}, bf16[256,256]{1,0:T(8,128)(2,1)}, u32[]{:S(2)}) copy-start(bf16[256,256]{1,0:T(8,128)(2,1)} %w_out.1) | copy-start | bytes 393220
  19.7 17.6 %collective-permute-start = (bf16[2,2,176,256]{3,2,1,0:T(8,128)(2,1)S(1)}, bf16[2,2,176,256]{3,2,1,0:T(8,128)(2,1)S(1)}, u32[]{:S(2)}, u32[]{:S(2)}) collective-permute-start(bf16[2,2,176,256]{3,2,1,0:T(8,128)(2,1)S(1)} %bitcast.8), channel_id=1, source_target_pairs={{16,1},{1,16},{18,3},{3,18},{20,5},{5,20},{22,7},{7,22},{24,9},{9,... | collective-permute-start | bytes 1081352 | tf_op jit(solution)/shard_map/ppermute | solution.py:506
  33.2 2.1 %copy-start.4 = (f32[256]{0:T(256)S(1)}, f32[256]{0:T(256)}, u32[]{:S(2)}) copy-start(f32[256]{0:T(256)} %param.25) | copy-start | bytes 3076
  33.2 7.8 %collective-permute-start.2 = (bf16[2,2,1,128,256]{4,3,2,1,0:T(8,128)(2,1)S(1)}, bf16[2,2,1,128,256]{4,3,2,1,0:T(8,128)(2,1)S(1)}, u32[]{:S(2)}, u32[]{:S(2)}) collective-permute-start(bf16[2,2,1,128,256]{4,3,2,1,0:T(8,128)(2,1)S(1)} %bitcast.15), channel_id=1, source_target_pairs={{16,1},{1,16},{18,3},{3,18},{20,5},{5,20},{22,7},{7,22},{24,9},{9,... | collective-permute-start | bytes 786440 | tf_op jit(solution)/shard_map/ppermute | solution.py:508
  37.4 3.6 %copy-start.2 = (bf16[256,256]{1,0:T(8,128)(2,1)S(1)}, bf16[256,256]{1,0:T(8,128)(2,1)}, u32[]{:S(2)}) copy-start(bf16[256,256]{1,0:T(8,128)(2,1)} %w_mix.1) | copy-start | bytes 393220

commit v5 on v4

--- a/solution.py
+++ b/solution.py
@@ -150,7 +150,7 @@
         copy.wait()
 
 
-def link_matrix(recv, partner, weight, edges, atoms):
+def link_factors(recv, partner, weight, edges, atoms):
     blocks = range(edges // atoms)
 
     def parts(index):
@@ -159,7 +159,7 @@
 
     into = blocked_onehot(*parts(recv), blocks, atoms)
     out_of = blocked_onehot(*parts(partner), blocks, atoms, weight)
-    return dot(out_of, into, NT).astype(BF16)
+    return out_of, into
 
 
 def scalar_columns(rows128, lines, kinds):
@@ -221,12 +221,19 @@
         for states in (mine, row_states(far))
     ]
     near[...] = rows[0]
+    held = None
+
+    def finish(tile, values, picks, reach):
+        pre[tile] = dot(values, picks) + columns[:, kinds : kinds + 1] * reach
+
     for tile in range(2):
         holder = core if tile == 0 else far
         recv, partner, weight, centre, cell, slot, reach, kind, _ = fields(
             pack[holder, core, atoms:], edges, trips, atoms, core
         )
-        links[tile] = link_matrix(recv, partner, weight, edges, atoms)
+        factors = link_factors(recv, partner, weight, edges, atoms)
+        if held is not None:
+            finish(*held)
         upper, lower = centre_split(centre_t, mine[1 + tile], kind, columns, kinds)
         span = slice(tile * atoms, (tile + 3) * atoms)
         values = jnp.concatenate([rows[0][:, span], rows[1][:, span], upper, lower], axis=1)
@@ -234,7 +241,9 @@
         picks = jnp.concatenate(
             [blocked_onehot(slot, cell, range(3, 9), atoms), pick_centre, pick_centre], axis=0
         )
-        pre[tile] = dot(values, picks) + columns[:, kinds : kinds + 1] * reach
+        links[tile] = dot(*factors, NT).astype(BF16)
+        held = (tile, values, picks, reach)
+    finish(*held)
 
 
 def inner_slots(tile):
@@ -272,12 +281,19 @@
         for row in (core, far)
     ]
     near_own = near_mine[...]
+    held = None
+
+    def finish(tile, values, picks, reach):
+        pre[tile] = dot(values, picks) + columns[:, kinds : kinds + 1] * reach
+
     for tile in range(2):
         holder = core if tile == 0 else far
         recv, partner, weight, centre, cell, slot, reach, kind, _ = fields(
             remote[holder, far, atoms:], edges, trips, atoms, core
         )
-        links[tile] = link_matrix(recv, partner, weight, edges, atoms)
+        factors = link_factors(recv, partner, weight, edges, atoms)
+        if held is not None:
+            finish(*held)
         states = remote[holder, far, 0:atoms]
         inner = [at - tile for at in inner_slots(tile)]
         span = slice(tile * atoms, (tile + 3) * atoms)
@@ -295,12 +311,14 @@
         picks = jnp.concatenate(
             [blocked_onehot(slot, cell, blocks, atoms), pick_centre, pick_centre], axis=0
         )
-        pre[tile] = dot(values, picks) + columns[:, kinds : kinds + 1] * reach
+        links[tile] = dot(*factors, NT).astype(BF16)
+        held = (tile, values, picks, reach)
         _, _, _, _, cell, slot, _, _, _ = fields(
             pack[holder, core, atoms:], edges, trips, atoms, core
         )
         picks = blocked_onehot(slot, cell, inner, atoms)
         pre_mine_out[tile] = pre_mine[tile] + dot(near_next, picks)
+    finish(*held)
 
 
 def edge_kernel(

time: 55.8 us -> 55.8 us (level)
  no operation moved by 1% of the time
where the time goes in v5:
time: 55.8 us; the launch traced here: 55.6 us
  blocking collectives  35.9 us (64%)
  Pallas kernels  9.57 us (17%)
  starting transfers between devices  8.66 us (16%)
  waiting for transfers between devices  1.26 us (2%)
    all_gather x3, blocking collectives, gathered(): return lax.all_gather(value, 'gy', axis_index_groups=chips)  30.6 us
    pallas_call x6, Pallas kernels, call(): pl.pallas_call(kernel, out_shape=outs, in_specs=specs or [VMEM] * len(ope...  9.57 us
    all_gather x1, blocking collectives, body(): lax.all_gather(side_out, 'gy', axis_index_groups=[list(pair) for pair in...  5.36 us
    ppermute x1, starting transfers between devices, body(): edge_col = lax.ppermute(state, 'gy', along_y)  4.58 us
    ppermute x1, starting transfers between devices, body(): remote = lax.ppermute(pack, both, along_x)  2.04 us
    ppermute x1, starting transfers between devices, body(): remote_edge = lax.ppermute(pair_edge, both, along_x)  2.04 us
    ppermute x1, waiting for transfers between devices, body(): remote_edge = lax.ppermute(pair_edge, both, along_x)  1.25 us
  transfers between devices with their start and end apart: 3, of which 1 were waited for; matrix products, arithmetic and copies ran while one was open for 0% of the time, Pallas kernels for 11%

profile of v5, /device:TPU:1, one launch (start us, length us, event | category | flops | bytes accessed | tf_op | source)
XLA Modules:
  0.0 55.6 jit_solution(10673082947537410381)
XLA Ops:
  0.0 4.6 %collective-permute-start.1 = (bf16[2,1,128,256]{3,2,1,0:T(8,128)(2,1)}, bf16[2,1,128,256]{3,2,1,0:T(8,128)(2,1)S(1)}, u32[]{:S(2)}, u32[]{:S(2)}) collective-permute-start(bf16[2,1,128,256]{3,2,1,0:T(8,128)(2,1)} %state_hbm.1), channel_id=1, source_target_pairs={{2,1},{1,2},{4,3},{3,4},{6,5},{5,6},{8,7},{7,8},{10,9},{9,10},{12,... | collective-permute-start | bytes 393224 | tf_op jit(solution)/shard_map/ppermute | solution.py:487
  4.6 1.8 %shard_map.145 = bf16[2,176,256]{2,1,0:T(8,128)(2,1)} custom-call(s32[2]{0:T(128)} %bitcast.20, s32[2]{0:T(128)} %bitcast.21, bf16[2,1,128,256]{3,2,1,0:T(8,128)(2,1)} %state_hbm.1, s32[2,1,2,512]{3,2,1,0:T(2,128)} %index_e_hbm.1, f32[2,1,512]{2,1,0:T(1,128)} %dist_hbm.1, s32[2,1,2,1024]{3,2,1,0:T(2,128)} %index_t_hbm.1, f32[2,1,1024]{2,1,0:T(1,128)} %cosine_hbm.1, ...), custom_call_target="tpu_custom_call" | custom-call | tf_op jit(solution)/shard_map/pallas_call | solution.py:433
  6.4 13.4 %all-gather = bf16[4,176,256]{2,1,0:T(8,128)(2,1)S(1)} all-gather(bf16[2,176,256]{2,1,0:T(8,128)(2,1)} %shard_map.145), channel_id=2, replica_groups={{0,1},{2,3},{4,5},{6,7},{8,9},{10,11},{12,13},{14,15},{16,17},{18,19},{..., dimensions={0}, use_global_device_ids=true | all-gather | bytes 540672 | tf_op jit(solution)/shard_map/all_gather | solution.py:482
  19.7 0.0 copy-start
  19.7 0.0 copy-start.1
  19.7 0.0 copy-start.3
  19.7 2.0 %collective-permute-start = (bf16[2,2,176,256]{3,2,1,0:T(8,128)(2,1)S(1)}, bf16[2,2,176,256]{3,2,1,0:T(8,128)(2,1)S(1)}, u32[]{:S(2)}, u32[]{:S(2)}) collective-permute-start(bf16[2,2,176,256]{3,2,1,0:T(8,128)(2,1)S(1)} %bitcast.8), channel_id=1, source_target_pairs={{16,1},{1,16},{18,3},{3,18},{20,5},{5,20},{22,7},{7,22},{24,9},{9,... | collective-permute-start | bytes 1081352 | tf_op jit(solution)/shard_map/ppermute | solution.py:524
  21.8 0.0 collective-permute-done.1.edge_col
  21.8 11.4 %all-gather.1 = bf16[4,1,128,256]{3,2,1,0:T(8,128)(2,1)S(1)} all-gather(bf16[2,1,128,256]{3,2,1,0:T(8,128)(2,1)S(1)} %collective-permute-done.1.edge_col), channel_id=3, replica_groups={{0,1},{2,3},{4,5},{6,7},{8,9},{10,11},{12,13},{14,15},{16,17},{18,19},{..., dimensions={0}, use_global_device_ids=true | all-gather | bytes 393216 | tf_op jit(solution)/shard_map/all_gather | solution.py:482
  33.2 0.0 copy-start.4
  33.2 2.0 %collective-permute-start.2 = (bf16[2,2,1,128,256]{4,3,2,1,0:T(8,128)(2,1)S(1)}, bf16[2,2,1,128,256]{4,3,2,1,0:T(8,128)(2,1)S(1)}, u32[]{:S(2)}, u32[]{:S(2)}) collective-permute-start(bf16[2,2,1,128,256]{4,3,2,1,0:T(8,128)(2,1)S(1)} %bitcast.15), channel_id=1, source_target_pairs={{16,1},{1,16},{18,3},{3,18},{20,5},{5,20},{22,7},{7,22},{24,9},{9,... | collective-permute-start | bytes 786440 | tf_op jit(solution)/shard_map/ppermute | solution.py:526
  35.2 0.0 copy-done
  35.3 0.0 copy-done.1
  35.3 0.0 copy-done.3
  35.3 0.0 copy-done.4
  35.3 2.1 %shard_map.146 = (bf16[2,512,512]{2,1,0:T(8,128)(2,1)S(1)}, f32[2,256,512]{2,1,0:T(8,128)S(1)}, bf16[256,512]{1,0:T(8,128)(2,1)S(1)}, bf16[256,256]{1,0:T(8,128)(2,1)S(1)}, f32[1,256]{1,0:T(1,128)S(1)}) custom-call(bf16[2,2,176,256]{3,2,1,0:T(8,128)(2,1)S(1)} %bitcast.9, bf16[2,1,128,256]{3,2,1,0:T(8,128)(2,1)S(1)} %collective-permute-done.1.edge_col, ...), custom_call_target="tpu_custom_call" | custom-call | tf_op jit(solution)/shard_map/pallas_call | solution.py:433
  37.4 0.0 collective-permute-done.remote
  37.4 0.0 copy-start.2
  37.4 2.3 %shard_map.147 = (bf16[2,512,512]{2,1,0:T(8,128)(2,1)S(1)}, f32[2,256,512]{2,1,0:T(8,128)S(1)}, f32[2,256,512]{2,1,0:T(8,128)S(1)}) custom-call(bf16[2,2,176,256]{3,2,1,0:T(8,128)(2,1)S(1)} %bitcast.10, bf16[2,2,176,256]{3,2,1,0:T(8,128)(2,1)S(1)} %collective-permute-done.remote, f32[2,256,512]{2,1,0:T(8,128)S(1)} %get-tuple-element.17.pre_mine, ...), custom_call_target="tpu_custom_call" | custom-call | tf_op jit(solution)/shard_map/pallas_call | solution.py:433
  39.8 1.3 %collective-permute-done.2.remote_edge = bf16[2,2,1,128,256]{4,3,2,1,0:T(8,128)(2,1)S(1)} collective-permute-done((bf16[2,2,1,128,256]{4,3,2,1,0:T(8,128)(2,1)S(1)}, bf16[2,2,1,128,256]{4,3,2,1,0:T(8,128)(2,1)S(1)}, u32[]{:S(2)}, u32[]{:S(2)}) %collective-permute-start.2) | collective-permute-done | bytes 262176 | tf_op jit(solution)/shard_map/ppermute | solution.py:526
  41.0 0.0 copy-done.2
  41.0 2.4 %shard_map.148 = (bf16[2,2,128,256]{3,2,1,0:T(8,128)(2,1)S(1)}, bf16[2,128,256]{2,1,0:T(8,128)(2,1)S(1)}, f32[2,128,256]{2,1,0:T(8,128)S(1)}) custom-call(bf16[2,2,176,256]{3,2,1,0:T(8,128)(2,1)S(1)} %bitcast.11, bf16[2,2,176,256]{3,2,1,0:T(8,128)(2,1)S(1)} %collective-permute-done.remote, ...), custom_call_target="tpu_custom_call" | custom-call | tf_op jit(solution)/shard_map/pallas_call | solution.py:433
  43.4 5.8 %all-gather.2 = bf16[4,2,128,256]{3,2,1,0:T(8,128)(2,1)S(1)} all-gather(bf16[2,2,128,256]{3,2,1,0:T(8,128)(2,1)S(1)} %get-tuple-element.23), channel_id=4, replica_groups={{0,1},{2,3},{4,5},{6,7},{8,9},{10,11},{12,13},{14,15},{16,17},{18,19},{..., dimensions={0}, use_global_device_ids=true | all-gather | bytes 786432 | tf_op jit(solution)/shard_map/all_gather | solution.py:482
  49.3 5.4 %all-gather.3 = bf16[4,128,256]{2,1,0:T(8,128)(2,1)S(1)} all-gather(bf16[2,128,256]{2,1,0:T(8,128)(2,1)S(1)} %shard_map.149), channel_id=5, replica_groups={{2,1},{4,3},{6,5},{8,7},{10,9},{12,11},{14,13},{0,15},{18,17},{20,19},{..., dimensions={0}, use_global_device_ids=true | all-gather | bytes 393216 | tf_op jit(solution)/shard_map/all_gather | solution.py:574
  54.6 0.9 %shard_map.150 = bf16[2,1,128,256]{3,2,1,0:T(8,128)(2,1)} custom-call(bf16[2,2,176,256]{3,2,1,0:T(8,128)(2,1)S(1)} %bitcast.12, f32[2,128,256]{2,1,0:T(8,128)S(1)} %get-tuple-element.22.owned, bf16[2,2,2,128,256]{4,3,2,1,0:T(8,128)(2,1)S(1)} %bitcast.14, bf16[2,2,128,256]{3,2,1,0:T(8,128)(2,1)S(1)} %bitcast.17, f32[1,256]{1,0:T(1,128)S(1)} %get-tuple-element.25.gain, ...), custom_call_target="tpu_custom_call" | custom-call | tf_op jit(solution)/shard_map/pallas_call | solution.py:433
  (1 shorter events, 0.0 us)
Async XLA Ops:
  0.0 21.8 %collective-permute-start.1 = (bf16[2,1,128,256]{3,2,1,0:T(8,128)(2,1)}, bf16[2,1,128,256]{3,2,1,0:T(8,128)(2,1)S(1)}, u32[]{:S(2)}, u32[]{:S(2)}) collective-permute-start(bf16[2,1,128,256]{3,2,1,0:T(8,128)(2,1)} %state_hbm.1), channel_id=1, source_target_pairs={{2,1},{1,2},{4,3},{3,4},{6,5},{5,6},{8,7},{7,8},{10,9},{9,10},{12,... | collective-permute-start | bytes 393224 | tf_op jit(solution)/shard_map/ppermute | solution.py:487
  19.7 15.5 %copy-start = (bf16[256,256]{1,0:T(8,128)(2,1)S(1)}, bf16[256,256]{1,0:T(8,128)(2,1)}, u32[]{:S(2)}) copy-start(bf16[256,256]{1,0:T(8,128)(2,1)} %w_neigh.5) | copy-start | bytes 393220
  19.7 15.5 %copy-start.1 = (bf16[256,256]{1,0:T(8,128)(2,1)S(1)}, bf16[256,256]{1,0:T(8,128)(2,1)}, u32[]{:S(2)}) copy-start(bf16[256,256]{1,0:T(8,128)(2,1)} %w_centre.3) | copy-start | bytes 393220
  19.7 15.5 %copy-start.3 = (bf16[256,256]{1,0:T(8,128)(2,1)S(1)}, bf16[256,256]{1,0:T(8,128)(2,1)}, u32[]{:S(2)}) copy-start(bf16[256,256]{1,0:T(8,128)(2,1)} %w_out.1) | copy-start | bytes 393220
  19.7 17.7 %collective-permute-start = (bf16[2,2,176,256]{3,2,1,0:T(8,128)(2,1)S(1)}, bf16[2,2,176,256]{3,2,1,0:T(8,128)(2,1)S(1)}, u32[]{:S(2)}, u32[]{:S(2)}) collective-permute-start(bf16[2,2,176,256]{3,2,1,0:T(8,128)(2,1)S(1)} %bitcast.8), channel_id=1, source_target_pairs={{16,1},{1,16},{18,3},{3,18},{20,5},{5,20},{22,7},{7,22},{24,9},{9,... | collective-permute-start | bytes 1081352 | tf_op jit(solution)/shard_map/ppermute | solution.py:524
  33.2 2.1 %copy-start.4 = (f32[256]{0:T(256)S(1)}, f32[256]{0:T(256)}, u32[]{:S(2)}) copy-start(f32[256]{0:T(256)} %param.25) | copy-start | bytes 3076
  33.2 7.8 %collective-permute-start.2 = (bf16[2,2,1,128,256]{4,3,2,1,0:T(8,128)(2,1)S(1)}, bf16[2,2,1,128,256]{4,3,2,1,0:T(8,128)(2,1)S(1)}, u32[]{:S(2)}, u32[]{:S(2)}) collective-permute-start(bf16[2,2,1,128,256]{4,3,2,1,0:T(8,128)(2,1)S(1)} %bitcast.15), channel_id=1, source_target_pairs={{16,1},{1,16},{18,3},{3,18},{20,5},{5,20},{22,7},{7,22},{24,9},{9,... | collective-permute-start | bytes 786440 | tf_op jit(solution)/shard_map/ppermute | solution.py:526
  37.4 3.6 %copy-start.2 = (bf16[256,256]{1,0:T(8,128)(2,1)S(1)}, bf16[256,256]{1,0:T(8,128)(2,1)}, u32[]{:S(2)}) copy-start(bf16[256,256]{1,0:T(8,128)(2,1)} %w_mix.1) | copy-start | bytes 393220
